TPU v7x, 32 devices: a whole 2x2x4 slice. The times are simulated.
32 devices in a mesh: seq: 16 (over z, y, x), batch: 2 (over core).
Axes of the slice: x: 2, y: 2, z: 4, core: 2. Of those that a mesh axis runs over, the one named last changes fastest.
Arguments:
- tokens: bfloat16 [2, 2048, 1024], P('batch', 'seq'), may hold values from -6 to 6
- out_grad: bfloat16 [2, 2048, 1024], P('batch', 'seq'), may hold values from -6 to 6
- norm1_gain: float32 [1024], replicated, may hold values from 0.5 to 1.5
- norm1_bias: float32 [1024], replicated, may hold values from -1.75 to 1.75
- value_weight: float32 [1024, 2048], P(('seq', 'batch')), may hold values from -0.1875 to 0.1875
- value_bias: float32 [2048], replicated, may hold values from -1.75 to 1.75
- ema_delta: float32 [1024, 16], replicated, may hold values from -11 to -2
- ema_alpha: float32 [1024, 16], replicated, may hold values from -1 to 2
- ema_beta: float32 [1024, 16], replicated, may hold values from -6 to 6
- ema_gamma: float32 [1024, 16], replicated, may hold values from -6 to 6
- ema_omega: float32 [1024], replicated, may hold values from -3 to 3
- base_weight: float32 [1024, 4224], P(('seq', 'batch')), may hold values from -0.1875 to 0.1875
- base_bias: float32 [4224], replicated, may hold values from -1.75 to 1.75
- shared_gamma: float32 [2, 128], replicated, may hold values from -12 to 12
- query_offset: float32 [128], replicated, may hold values from -6 to 6
- position_bias: float32 [128], replicated, may hold values from -6 to 6
- proj_weight: float32 [2048, 1024], P(('seq', 'batch')), may hold values from -0.5 to 0.5
- proj_bias: float32 [1024], replicated, may hold values from -1.75 to 1.75
- norm2_gain: float32 [1024], replicated, may hold values from 0.5 to 1.5
- norm2_bias: float32 [1024], replicated, may hold values from -1.75 to 1.75
- ffn1_weight: float32 [1024, 4096], P(('seq', 'batch')), may hold values from -0.1875 to 0.1875
- ffn1_bias: float32 [4096], replicated, may hold values from -1.75 to 1.75
- ffn2_weight: float32 [4096, 1024], P(('seq', 'batch')), may hold values from -0.09375 to 0.09375
- ffn2_bias: float32 [1024], replicated, may hold values from -1.75 to 1.75
Outputs:
- block_out: bfloat16 [2, 2048, 1024], P('batch', 'seq')
- tokens_grad: bfloat16 [2, 2048, 1024], P('batch', 'seq')
- dnorm1_gain: float32 [1024], replicated
- dnorm1_bias: float32 [1024], replicated
- dvalue_weight: float32 [1024, 2048], P(('seq', 'batch'))
- dvalue_bias: float32 [2048], replicated
- dema_delta: float32 [1024, 16], replicated
- dema_alpha: float32 [1024, 16], replicated
- dema_beta: float32 [1024, 16], replicated
- dema_gamma: float32 [1024, 16], replicated
- dema_omega: float32 [1024], replicated
- dbase_weight: float32 [1024, 4224], P(('seq', 'batch'))
- dbase_bias: float32 [4224], replicated
- dshared_gamma: float32 [2, 128], replicated
- dquery_offset: float32 [128], replicated
- dposition_bias: float32 [128], replicated
- dproj_weight: float32 [2048, 1024], P(('seq', 'batch'))
- dproj_bias: float32 [1024], replicated
- dnorm2_gain: float32 [1024], replicated
- dnorm2_bias: float32 [1024], replicated
- dffn1_weight: float32 [1024, 4096], P(('seq', 'batch'))
- dffn1_bias: float32 [4096], replicated
- dffn2_weight: float32 [4096, 1024], P(('seq', 'batch'))
- dffn2_bias: float32 [1024], replicated
All inputs are finite; a program needn't handle non-finite values.
Results may differ from a plain program's by a relative error of at most 0.02.
Values may be sent and summed in bfloat16 or wider, within the bound.
A program may use at most 320 MiB of HBM per device.

v0:
```python
import jax
import jax.numpy as jnp
from jax import lax
from jax.sharding import PartitionSpec as P

D = 1024
ZD = 128
VD = 2048
NDIM = 16


precise = lax.Precision.HIGHEST


def entering(part, axis, combine, identity):
    place = lax.axis_index(axis)
    gathered = jax.tree.map(lambda a: lax.all_gather(a, axis), part)
    state = jax.tree.map(lambda a, e: jnp.zeros_like(a) + jnp.asarray(e, a.dtype), part, identity)

    def one(step, state):
        return combine(
            state, jax.tree.map(lambda a: lax.dynamic_index_in_dim(a, step, 0, False), gathered)
        )

    return lax.fori_loop(0, place, one, state)


def prefix_2(value, axis, combine, identity):
    size, index = (lax.axis_size(axis), lax.axis_index(axis))
    everything = jax.tree.map(
        lambda part, kind: lax.all_gather(part.astype(kind), axis),
        value,
        jax.tree.map(lambda a: jnp.bfloat16 if a.dtype == jnp.float32 else a.dtype, value),
    )
    start = jax.tree.map(
        lambda part, zero: jnp.broadcast_to(jnp.asarray(zero, part.dtype), part.shape),
        value,
        identity,
    )

    def step(k, before):
        at = size - 1 - k
        reached = at > index
        new = combine(
            before, jax.tree.map(lambda part, own: part[at].astype(own.dtype), everything, value)
        )
        return jax.tree.map(lambda a, b: jnp.where(reached, a, b), new, before)

    return lax.fori_loop(0, size, step, start)


def layer_norm(values, norm_gain, norm_bias):
    center = values - jnp.mean(values, axis=-1, keepdims=True)
    spread = jnp.mean(center * center, axis=-1, keepdims=True)
    return center * lax.rsqrt(spread + 1e-05) * norm_gain + norm_bias


def decay_tables(delta, alpha):
    input_rate = jax.nn.sigmoid(delta)
    damping = jax.nn.sigmoid(alpha)
    return (input_rate, jnp.log1p(-input_rate * damping))


def toeplitz_rows(kern_part):
    chans = kern_part.shape[0]
    block_len = kern_part.shape[1]
    wrapped = jnp.concatenate(
        [kern_part[:, :1], jnp.zeros((chans, block_len), kern_part.dtype), kern_part[:, :0:-1]],
        axis=1,
    )
    tiled = jnp.tile(wrapped, (1, block_len))[:, : block_len * (2 * block_len - 1)]
    return tiled.reshape(chans, block_len, 2 * block_len - 1)[:, :, :block_len]


def local_conv(normed3, kernel):
    block_len = normed3.shape[1]
    blocks = normed3.shape[2] // 128
    kern_blocks = kernel.reshape(blocks, 128, block_len)
    data_blocks = normed3.reshape(normed3.shape[0], block_len, blocks, 128).transpose(2, 0, 1, 3)

    def one_block(block_pair):
        kern_part, data_part = block_pair
        toeplitz = toeplitz_rows(kern_part)
        return jnp.einsum("dts,bsd->btd", toeplitz, data_part, precision=precise)

    result = lax.map(one_block, (kern_blocks, data_blocks))
    return result.transpose(1, 2, 0, 3).reshape(normed3.shape)


def ema_terms(normed3, delta, alpha, beta, gamma, omega, incoming):
    block_len = normed3.shape[1]
    input_rate, log_decay = decay_tables(delta, alpha)
    step_index = jnp.arange(block_len, dtype=jnp.float32)
    ema_scale = NDIM ** (-0.5)
    powers = jnp.exp(log_decay[:, :, None] * step_index)
    kernel = ema_scale * jnp.einsum(
        "dj,djk->dk", gamma * input_rate * beta, powers, precision=precise
    )
    convolved = local_conv(normed3, kernel)
    carry_table = (
        ema_scale * gamma[:, :, None] * jnp.exp(log_decay[:, :, None] * (step_index + 1.0))
    )
    carried = jnp.einsum("djt,bdj->btd", carry_table, incoming, precision=precise)
    return convolved + carried + omega * normed3


def ema_ends(normed3, delta, alpha, beta):
    block_len = normed3.shape[1]
    input_rate, log_decay = decay_tables(delta, alpha)
    step_index = jnp.arange(block_len, dtype=jnp.float32)
    end_table = (input_rate * beta)[:, :, None] * jnp.exp(
        log_decay[:, :, None] * (block_len - 1.0 - step_index)
    )
    end_states = jnp.einsum("djs,bsd->bdj", end_table, normed3, precision=precise)
    return (jnp.exp(log_decay * block_len), end_states)


def rel_table(position_bias):
    step_index = jnp.arange(position_bias.shape[0])
    offsets = step_index[:, None] - step_index[None, :]
    return jnp.where(offsets >= 0, position_bias[jnp.maximum(offsets, 0)], 0.0)


def masked_softmax(scores):
    step_index = jnp.arange(scores.shape[-1])
    causal = step_index[:, None] >= step_index[None, :]
    masked = jnp.where(causal, scores, -jnp.inf)
    row_top = jnp.max(masked, axis=-1, keepdims=True)
    expo_vals = jnp.exp(masked - row_top)
    return expo_vals / jnp.sum(expo_vals, axis=-1, keepdims=True)


def silu_slope(values):
    logistic = jax.nn.sigmoid(values)
    return logistic * (1.0 + values * (1.0 - logistic))


def matmul(left_mat, right_mat):
    return jnp.dot(left_mat, right_mat, preferred_element_type=jnp.float32)


def left_product(left_mat, right_mat):
    return lax.dot_general(
        left_mat, right_mat, (((0,), (0,)), ((), ())), preferred_element_type=jnp.float32
    )


def right_product(left_mat, right_mat):
    return lax.dot_general(
        left_mat, right_mat, (((1,), (1,)), ((), ())), preferred_element_type=jnp.float32
    )


def column_sums(values):
    return jnp.sum(values.astype(jnp.float32), axis=0)


def shards(
    tokens,
    out_grad,
    norm1_gain,
    norm1_bias,
    value_weight,
    value_bias,
    ema_delta,
    ema_alpha,
    ema_beta,
    ema_gamma,
    ema_omega,
    base_weight,
    base_bias,
    shared_gamma,
    query_offset,
    position_bias,
    proj_weight,
    proj_bias,
    norm2_gain,
    norm2_bias,
    ffn1_weight,
    ffn1_bias,
    ffn2_weight,
    ffn2_bias,
):
    seq_local, block_len, _ = tokens.shape
    row_count = seq_local * block_len
    gathered = (
        lax.all_gather(value_weight.astype(jnp.bfloat16), ("seq", "batch"), axis=0, tiled=True),
        lax.all_gather(base_weight.astype(jnp.bfloat16), ("seq", "batch"), axis=0, tiled=True),
        lax.all_gather(proj_weight.astype(jnp.bfloat16), ("seq", "batch"), axis=0, tiled=True),
        lax.all_gather(ffn1_weight.astype(jnp.bfloat16), ("seq", "batch"), axis=0, tiled=True),
        lax.all_gather(ffn2_weight.astype(jnp.bfloat16), ("seq", "batch"), axis=0, tiled=True),
    )
    value_full, base_full, proj_full, ffn1_full, ffn2_full = gathered
    _, log_decay = decay_tables(ema_delta, ema_alpha)
    block_log = log_decay * block_len

    def chain_step(earlier_pair, later_pair):
        carried = earlier_pair[1] * jnp.exp(block_log * later_pair[0][0])
        return (earlier_pair[0] + later_pair[0], carried + later_pair[1])

    one_block = jnp.ones((1,), jnp.float32)
    no_block = jnp.zeros((1,), jnp.float32)
    tokens_flat = tokens.astype(jnp.float32).reshape(row_count, D)
    normed, norm1_back = jax.vjp(layer_norm, tokens_flat, norm1_gain, norm1_bias)
    normed_low = normed.astype(jnp.bfloat16)
    value_pre = matmul(normed_low, value_full) + value_bias
    value_low = jax.nn.silu(value_pre).astype(jnp.bfloat16)
    normed3 = normed.reshape(seq_local, block_len, D)
    (whole_decay, end_states), ends_back = jax.vjp(
        ema_ends, normed3, ema_delta, ema_alpha, ema_beta
    )
    prefix = entering(
        (one_block, end_states), "seq", chain_step, (no_block, jnp.zeros_like(end_states))
    )
    incoming = prefix[1]
    ema_out, ema_back = jax.vjp(
        ema_terms, normed3, ema_delta, ema_alpha, ema_beta, ema_gamma, ema_omega, incoming
    )
    ema_flat = ema_out.reshape(row_count, D)
    mixed_low = jax.nn.silu(ema_flat).astype(jnp.bfloat16)
    base_pre = matmul(mixed_low, base_full) + base_bias
    update = jax.nn.sigmoid(base_pre[:, :D])
    shared_pre = base_pre[:, D : D + ZD + VD]
    shared_reset = jax.nn.silu(shared_pre)
    shared = shared_reset[:, :ZD]
    reset_gate = shared_reset[:, ZD:]
    hidden_x = base_pre[:, D + ZD + VD :]
    queries = (
        (shared * shared_gamma[0] + query_offset)
        .astype(jnp.bfloat16)
        .reshape(seq_local, block_len, ZD)
    )
    key_rows = (shared * shared_gamma[1]).astype(jnp.bfloat16).reshape(seq_local, block_len, ZD)
    position, position_back = jax.vjp(rel_table, position_bias)
    scores = (
        jnp.einsum("bik,bjk->bij", queries, key_rows, preferred_element_type=jnp.float32)
        * ZD ** (-0.5)
        + position
    )
    attn = masked_softmax(scores)
    attn_low = attn.astype(jnp.bfloat16)
    values3 = value_low.reshape(seq_local, block_len, VD)
    attended = jnp.einsum(
        "bij,bjv->biv", attn_low, values3, preferred_element_type=jnp.float32
    ).reshape(row_count, VD)
    gated_low = (attended * reset_gate).astype(jnp.bfloat16)
    proj_pre = matmul(gated_low, proj_full) + proj_bias
    hidden_sum = hidden_x + proj_pre
    hidden = jax.nn.silu(hidden_sum)
    first_out = tokens_flat + update * (hidden - tokens_flat)
    normed_two, norm2_back = jax.vjp(layer_norm, first_out, norm2_gain, norm2_bias)
    normed_two_low = normed_two.astype(jnp.bfloat16)
    ffn_pre = matmul(normed_two_low, ffn1_full) + ffn1_bias
    ffn_low = jax.nn.silu(ffn_pre).astype(jnp.bfloat16)
    ffn_out = matmul(ffn_low, ffn2_full) + ffn2_bias
    block_out = (first_out + ffn_out).astype(jnp.bfloat16).reshape(seq_local, block_len, D)
    grad_ffn2 = out_grad.reshape(row_count, D)
    dffn2_weight = left_product(ffn_low, grad_ffn2)
    dffn2_bias = column_sums(grad_ffn2)
    grad_ffn1 = (right_product(grad_ffn2, ffn2_full) * silu_slope(ffn_pre)).astype(jnp.bfloat16)
    dffn1_weight = left_product(normed_two_low, grad_ffn1)
    dffn1_bias = column_sums(grad_ffn1)
    grad_first_norm, dnorm2_gain, dnorm2_bias = norm2_back(right_product(grad_ffn1, ffn1_full))
    grad_first = grad_ffn2.astype(jnp.float32) + grad_first_norm
    grad_skip = grad_first * (1.0 - update)
    grad_update = grad_first * (hidden - tokens_flat)
    grad_hidden = grad_first * update * silu_slope(hidden_sum)
    grad_proj = grad_hidden.astype(jnp.bfloat16)
    dproj_weight = left_product(gated_low, grad_proj)
    dproj_bias = column_sums(grad_proj)
    grad_gated = right_product(grad_proj, proj_full)
    grad_attended = (grad_gated * reset_gate).astype(jnp.bfloat16).reshape(seq_local, block_len, VD)
    grad_reset = grad_gated * attended
    grad_attn = jnp.einsum(
        "biv,bjv->bij", grad_attended, values3, preferred_element_type=jnp.float32
    )
    grad_values = jnp.einsum(
        "bij,biv->bjv", attn_low, grad_attended, preferred_element_type=jnp.float32
    ).reshape(row_count, VD)
    grad_scores = (attn * (grad_attn - jnp.sum(grad_attn * attn, axis=-1, keepdims=True))).astype(
        jnp.bfloat16
    )
    (dposition_bias,) = position_back(jnp.sum(grad_scores.astype(jnp.float32), axis=0))
    grad_queries = jnp.einsum(
        "bij,bjk->bik", grad_scores, key_rows, preferred_element_type=jnp.float32
    ).reshape(row_count, ZD) * ZD ** (-0.5)
    grad_keys = jnp.einsum(
        "bij,bik->bjk", grad_scores, queries, preferred_element_type=jnp.float32
    ).reshape(row_count, ZD) * ZD ** (-0.5)
    dshared_gamma = jnp.stack(
        [jnp.sum(grad_queries * shared, axis=0), jnp.sum(grad_keys * shared, axis=0)]
    )
    dquery_offset = jnp.sum(grad_queries, axis=0)
    grad_shared = grad_queries * shared_gamma[0] + grad_keys * shared_gamma[1]
    grad_shared_pre = jnp.concatenate([grad_shared, grad_reset], axis=1) * silu_slope(shared_pre)
    grad_update_pre = grad_update * update * (1.0 - update)
    grad_base = jnp.concatenate([grad_update_pre, grad_shared_pre, grad_hidden], axis=1).astype(
        jnp.bfloat16
    )
    dbase_weight = left_product(mixed_low, grad_base)
    dbase_bias = column_sums(grad_base)
    grad_ema = right_product(grad_base, base_full) * silu_slope(ema_flat)
    grad_value_pre = (grad_values * silu_slope(value_pre)).astype(jnp.bfloat16)
    dvalue_weight = left_product(normed_low, grad_value_pre)
    dvalue_bias = column_sums(grad_value_pre)
    grad_normed = right_product(grad_value_pre, value_full)
    grad_normed_ema, delta_part, alpha_part, beta_part, dema_gamma, dema_omega, grad_incoming = (
        ema_back(grad_ema.reshape(seq_local, block_len, D))
    )
    suffix = prefix_2(
        (one_block, grad_incoming), "seq", chain_step, (no_block, jnp.zeros_like(grad_incoming))
    )
    grad_ends = suffix[1]
    grad_whole = jnp.sum(grad_ends * incoming, axis=0)
    grad_normed_ends, delta_rest, alpha_rest, beta_rest = ends_back((grad_whole, grad_ends))
    dema_delta = delta_part + delta_rest
    dema_alpha = alpha_part + alpha_rest
    dema_beta = beta_part + beta_rest
    grad_normed = grad_normed + (grad_normed_ema + grad_normed_ends).reshape(row_count, D)
    grad_tokens_norm, dnorm1_gain, dnorm1_bias = norm1_back(grad_normed)
    tokens_grad = (
        (grad_skip + grad_tokens_norm).astype(jnp.bfloat16).reshape(seq_local, block_len, D)
    )
    small_sums = lax.psum(
        (
            dnorm1_gain,
            dnorm1_bias,
            dvalue_bias,
            dema_delta,
            dema_alpha,
            dema_beta,
            dema_gamma,
            dema_omega,
            dbase_bias,
            dshared_gamma,
            dquery_offset,
            dposition_bias,
            dproj_bias,
            dnorm2_gain,
            dnorm2_bias,
            dffn1_bias,
            dffn2_bias,
        ),
        ("seq", "batch"),
    )
    reduced = (
        lax.psum_scatter(dvalue_weight, ("seq", "batch"), scatter_dimension=0, tiled=True),
        lax.psum_scatter(dbase_weight, ("seq", "batch"), scatter_dimension=0, tiled=True),
        lax.psum_scatter(dproj_weight, ("seq", "batch"), scatter_dimension=0, tiled=True),
        lax.psum_scatter(dffn1_weight, ("seq", "batch"), scatter_dimension=0, tiled=True),
        lax.psum_scatter(dffn2_weight, ("seq", "batch"), scatter_dimension=0, tiled=True),
    )
    return (
        block_out,
        tokens_grad,
        small_sums[0],
        small_sums[1],
        reduced[0],
        small_sums[2],
        small_sums[3],
        small_sums[4],
        small_sums[5],
        small_sums[6],
        small_sums[7],
        reduced[1],
        small_sums[8],
        small_sums[9],
        small_sums[10],
        small_sums[11],
        reduced[2],
        small_sums[12],
        small_sums[13],
        small_sums[14],
        reduced[3],
        small_sums[15],
        reduced[4],
        small_sums[16],
    )


def solution(mesh):
    in_specs = (
        P("batch", "seq", None),
        P("batch", "seq", None),
        P(),
        P(),
        P(("seq", "batch"), None),
        P(),
        P(),
        P(),
        P(),
        P(),
        P(),
        P(("seq", "batch"), None),
        P(),
        P(),
        P(),
        P(),
        P(("seq", "batch"), None),
        P(),
        P(),
        P(),
        P(("seq", "batch"), None),
        P(),
        P(("seq", "batch"), None),
        P(),
    )
    out_specs = (
        P("batch", "seq", None),
        P("batch", "seq", None),
        P(),
        P(),
        P(("seq", "batch"), None),
        P(),
        P(),
        P(),
        P(),
        P(),
        P(),
        P(("seq", "batch"), None),
        P(),
        P(),
        P(),
        P(),
        P(("seq", "batch"), None),
        P(),
        P(),
        P(),
        P(("seq", "batch"), None),
        P(),
        P(("seq", "batch"), None),
        P(),
    )
    return jax.shard_map(shards, mesh=mesh, in_specs=in_specs, out_specs=out_specs, check_vma=False)
```

profile of v0, /device:TPU:27, one launch (start us, length us, event | category | flops | bytes accessed | tf_op | source)
XLA Modules:
  0.0 2885.2 jit_solution(14023228159101760518)
XLA Ops:
  33.4 27.8 all-reduce.3
  72.7 32.5 %all-reduce.4 = bf16[16]{0:T(256)(128)(2,1)} all-reduce(bf16[16]{0:T(256)(128)(2,1)S(1)} %dynamic-update-slice.1), channel_id=1, replica_groups=mesh['seq'=16,'batch'=2] {'seq'}, use_global_device_ids=true, to_apply=%add.4 | all-reduce | flops 16 | bytes 64
  105.5 168.0 %gather_fusion = f32[16384]{0:T(1024)} fusion(f32[128]{0:T(128)S(1)} %copy-done, s32[16384]{0:T(1024)S(1)} %broadcast_clamp_fusion), kind=kCustom, calls=%fused_computation | custom fusion | bytes 196608 | tf_op jit(solution)/shard_map/jvp()/gather | solution.py:121
  273.6 568.4 %while.56 = (s32[]{:T(128)}, f32[8,1,128,128]{3,2,1,0:T(8,128)S(1)}, f32[8,128,128,128]{3,2,1,0:T(8,128)}, f32[8,1,128,128]{3,2,1,0:T(8,128)S(1)}, f32[8,128,128...) while((s32[]{:T(128)}, f32[8,1,128,128]{3,2,1,0:T(8,128)S(1)}, f32[8,128,128,128]{3,2,1,0:T(8,128)}, ...), condition=%wide.region_3.4_spmd, body=%wide.region_2.3_spmd.sunk | while | flops 4243458 | bytes 143722096 | solution.py:86
  302.2 29.0 %reshape.612 = f32[128,128,255]{2,1,0:T(8,128)} reshape(f32[128,32640]{1,0:T(8,128)} %slice.122) | data formatting | bytes 33423360 | tf_op jit(solution)/shard_map/jvp()/while/body/eval_jaxpr/reshape | solution.py:72
  373.3 28.9 %reshape.612 = f32[128,128,255]{2,1,0:T(8,128)} reshape(f32[128,32640]{1,0:T(8,128)} %slice.122) | data formatting | bytes 33423360 | tf_op jit(solution)/shard_map/jvp()/while/body/eval_jaxpr/reshape | solution.py:72
  444.5 28.9 %reshape.612 = f32[128,128,255]{2,1,0:T(8,128)} reshape(f32[128,32640]{1,0:T(8,128)} %slice.122) | data formatting | bytes 33423360 | tf_op jit(solution)/shard_map/jvp()/while/body/eval_jaxpr/reshape | solution.py:72
  515.5 28.9 %reshape.612 = f32[128,128,255]{2,1,0:T(8,128)} reshape(f32[128,32640]{1,0:T(8,128)} %slice.122) | data formatting | bytes 33423360 | tf_op jit(solution)/shard_map/jvp()/while/body/eval_jaxpr/reshape | solution.py:72
  586.5 28.9 %reshape.612 = f32[128,128,255]{2,1,0:T(8,128)} reshape(f32[128,32640]{1,0:T(8,128)} %slice.122) | data formatting | bytes 33423360 | tf_op jit(solution)/shard_map/jvp()/while/body/eval_jaxpr/reshape | solution.py:72
  657.4 28.9 %reshape.612 = f32[128,128,255]{2,1,0:T(8,128)} reshape(f32[128,32640]{1,0:T(8,128)} %slice.122) | data formatting | bytes 33423360 | tf_op jit(solution)/shard_map/jvp()/while/body/eval_jaxpr/reshape | solution.py:72
  728.4 28.9 %reshape.612 = f32[128,128,255]{2,1,0:T(8,128)} reshape(f32[128,32640]{1,0:T(8,128)} %slice.122) | data formatting | bytes 33423360 | tf_op jit(solution)/shard_map/jvp()/while/body/eval_jaxpr/reshape | solution.py:72
  799.4 28.9 %reshape.612 = f32[128,128,255]{2,1,0:T(8,128)} reshape(f32[128,32640]{1,0:T(8,128)} %slice.122) | data formatting | bytes 33423360 | tf_op jit(solution)/shard_map/jvp()/while/body/eval_jaxpr/reshape | solution.py:72
  922.9 530.1 %while.58 = (s32[]{:T(128)}, f32[8,128,128]{2,1,0:T(8,128)S(1)}, f32[8,1,128,128]{3,2,1,0:T(8,128)S(1)}, f32[8,1,128,128]{2,3,1,0:T(8,128)S(1)}, f32[8,1,128,128...) while((s32[]{:T(128)}, f32[8,128,128]{2,1,0:T(8,128)S(1)}, ...), condition=%wide.region_15.16_spmd, body=%wide.region_13.15_spmd.sunk | while | flops 31457284 | bytes 160758400 | solution.py:86
  1464.1 35.2 %all-gather.1 = bf16[16384,16]{0,1:T(8,128)(2,1)S(1)} all-gather(bf16[1024,16]{0,1:T(8,128)(2,1)S(1)} %copy.164), channel_id=3, replica_groups=mesh['seq'=16,'batch'=2] {'seq'}, dimensions={0}, use_global_device_ids=true | all-gather | bytes 557056 | tf_op jit(solution)/shard_map/all_gather | solution.py:31
  1499.9 21.2 while.59
  1522.3 28.7 fusion.12
  1584.4 114.5 %scatter_custom_fusion = f32[128]{0:T(128)} fusion(s32[16384]{0:T(1024)} %maximum_bitcast_fusion, f32[16384]{0:T(1024)} %get-tuple-element.552, f32[]{:T(128)} %constant.182.clone.1), kind=kCustom, calls=%fused_computation.203 | custom fusion | flops 16384 | bytes 1024 | tf_op jit(solution)/shard_map/transpose(jvp())/scatter-add | solution.py:121
  1746.3 103.9 %all-reduce.10.cloned.1.call-done = (f32[1024]{0:T(1024)}, f32[1024]{0:T(1024)}, f32[2048]{0:T(1024)}, f32[1024]{0:T(1024)}, f32[4224]{0:T(1024)}, /*index=5*/f3...) async-done(((f32[1024]{0:T(1024)}, f32[1024]{0:T(1024)}, ...) | async-done | bytes 72208 | tf_op jit(solution)/shard_map/psum | solution.py:324
  1850.2 134.2 %all-reduce.12.cloned.1.call-done = (f32[1024,16]{0,1:T(8,128)}, f32[1024,16]{0,1:T(8,128)}, f32[1024,16]{0,1:T(8,128)}, f32[1024,16]{0,1:T(8,128)}) async-done(((f32[1024,16]{0,1:T(8,128)}, f32[1024,16]{0,1:T(8,128)}, f32[1024,16]{0,1:T(8,128)}, f32[1024,16]{0,1:T(8,128)}), (f32[1024,16]{0,1:T(8,128)}, f32[1024,16]{0,1:T(8,128)}, f32[1024,16]{0,1:T(8,128)}, ...) | async-done | bytes 262160 | tf_op jit(solution)/shard_map/psum | solution.py:324
  1984.4 140.4 %reduce-scatter.10.cloned.1.call-done = f32[64,1024]{1,0:T(8,128)} async-done(((f32[2048,1024]{1,0:T(8,128)}), f32[64,1024]{1,0:T(8,128)}) %reduce-scatter.10.cloned.1.call-update) | async-done | bytes 262160 | tf_op jit(solution)/shard_map/reduce_scatter | solution.py:349
  2124.8 147.4 %reduce-scatter.6.cloned.1.call-done = f32[32,2048]{1,0:T(8,128)} async-done(((f32[1024,2048]{1,0:T(8,128)}), f32[32,2048]{1,0:T(8,128)}) %reduce-scatter.6.cloned.1.call-update) | async-done | bytes 262160 | tf_op jit(solution)/shard_map/reduce_scatter | solution.py:347
  2272.2 209.2 %reduce-scatter.8.cloned.1.call-done = f32[32,4224]{1,0:T(8,128)} async-done(((f32[1024,4224]{1,0:T(8,128)}), f32[32,4224]{1,0:T(8,128)}) %reduce-scatter.8.cloned.1.call-update) | async-done | bytes 540688 | tf_op jit(solution)/shard_map/reduce_scatter | solution.py:348
  2481.4 186.8 %reduce-scatter.12.cloned.1.call-done = f32[32,4096]{1,0:T(8,128)} async-done(((f32[1024,4096]{1,0:T(8,128)}), f32[32,4096]{1,0:T(8,128)}) %reduce-scatter.12.cloned.1.call-update) | async-done | bytes 524304 | tf_op jit(solution)/shard_map/reduce_scatter | solution.py:350
  2668.2 188.0 %reduce-scatter.14.cloned.1.call-done = f32[128,1024]{1,0:T(8,128)} async-done(((f32[4096,1024]{1,0:T(8,128)}), f32[128,1024]{1,0:T(8,128)}) %reduce-scatter.14.cloned.1.call-update) | async-done | bytes 524304 | tf_op jit(solution)/shard_map/reduce_scatter | solution.py:351
  (702 shorter events, 1125.9 us)
Async XLA Ops:
  7.3 834.7 %all-gather.19.cloned.1.call-start = ((), (), s32[]{:S(2)}) async-start(), calls=%async_computation.15 | async-start | bytes 1114112 | tf_op jit(solution)/shard_map/all_gather | solution.py:17
  25.4 846.9 %all-gather.11.cloned.1.call-start = ((), (), s32[]{:S(2)}) async-start(), calls=%async_computation.6 | async-start | bytes 4325376 | tf_op jit(solution)/shard_map/all_gather | solution.py:187
  26.1 850.4 %all-gather.9.cloned.1.call-start = ((), (), s32[]{:S(2)}) async-start(), calls=%async_computation.5 | async-start | bytes 8921088 | tf_op jit(solution)/shard_map/all_gather | solution.py:188
  26.9 857.7 %all-gather.13.cloned.1.call-start = ((), (), s32[]{:S(2)}) async-start(), calls=%async_computation.7 | async-start | bytes 4325376 | tf_op jit(solution)/shard_map/all_gather | solution.py:189
  28.6 862.9 %all-gather.15.cloned.1.call-start = ((), (), s32[]{:S(2)}) async-start(), calls=%async_computation.8 | async-start | bytes 8650752 | tf_op jit(solution)/shard_map/all_gather | solution.py:190
  29.4 868.3 %all-gather.17.cloned.1.call-start = ((), (), s32[]{:S(2)}) async-start(), calls=%async_computation.9 | async-start | bytes 8650752 | tf_op jit(solution)/shard_map/all_gather | solution.py:191
  30.3 1820.0 %all-reduce.10.cloned.1.call-start = ((), (), s32[]{:S(2)}) async-start(), calls=%async_computation.16 | async-start | bytes 151552 | tf_op jit(solution)/shard_map/psum | solution.py:324
  273.5 570.6 %copy-start.14 = (f32[1024,16]{0,1:T(8,128)S(1)}, f32[1024,16]{0,1:T(8,128)}, u32[]{:S(2)}) copy-start(f32[1024,16]{0,1:T(8,128)} %get-tuple-element.793) | copy-start | bytes 196612
  273.5 570.6 %copy-start.111 = (f32[16]{0:T(128)S(1)}, f32[16]{0:T(128)}, u32[]{:S(2)}) copy-start(f32[16]{0:T(128)} %all-reduce.3) | copy-start | bytes 196
  273.5 588.5 %copy-start.49 = (f32[1024,16]{1,0:T(8,128)S(1)}, f32[1024,16]{1,0:T(8,128)}, u32[]{:S(2)}) copy-start(f32[1024,16]{1,0:T(8,128)} %copy-done.48) | copy-start | bytes 196612
  273.5 588.5 %copy-start.52 = (f32[1024,16]{1,0:T(8,128)S(1)}, f32[1024,16]{1,0:T(8,128)}, u32[]{:S(2)}) copy-start(f32[1024,16]{1,0:T(8,128)} %copy.120) | copy-start | bytes 196612
  922.4 532.8 %copy-start.50 = (f32[1024,16]{1,0:T(8,128)S(1)}, f32[1024,16]{1,0:T(8,128)}, u32[]{:S(2)}) copy-start(f32[1024,16]{1,0:T(8,128)} %copy-done.48) | copy-start | bytes 196612
  922.4 532.8 %copy-start.113 = (f32[128]{0:T(128)S(1)}, f32[128]{0:T(128)}, u32[]{:S(2)}) copy-start(f32[128]{0:T(128)} %get-tuple-element.593) | copy-start | bytes 1540
  1572.6 126.3 %copy-start.66 = (f32[1024,16]{0,1:T(8,128)S(1)}, f32[1024,16]{0,1:T(8,128)}, u32[]{:S(2)}) copy-start(f32[1024,16]{0,1:T(8,128)} %param.38) | copy-start | bytes 196612
  1572.6 126.3 %copy-start.67 = (f32[1024,16]{0,1:T(8,128)S(1)}, f32[1024,16]{0,1:T(8,128)}, u32[]{:S(2)}) copy-start(f32[1024,16]{0,1:T(8,128)} %param.41) | copy-start | bytes 196612
  1572.6 127.3 %copy-start.17 = (bf16[128,1024]{1,0:T(8,128)(2,1)S(1)}, bf16[128,1024]{1,0:T(8,128)(2,1)}, u32[]{:S(2)}) copy-start(bf16[128,1024]{1,0:T(8,128)(2,1)} %copy-done.16) | copy-start | bytes 786436
  1572.6 127.3 %copy-start.19 = (bf16[128,2048]{1,0:T(8,128)(2,1)S(1)}, bf16[128,2048]{1,0:T(8,128)(2,1)}, u32[]{:S(2)}) copy-start(bf16[128,2048]{1,0:T(8,128)(2,1)} %copy-done.18) | copy-start | bytes 1572868
  1698.9 285.6 %all-reduce.12.cloned.1.call-start = ((), (), s32[]{:S(2)}) async-start(), calls=%async_computation.17 | async-start | bytes 524288 | tf_op jit(solution)/shard_map/psum | solution.py:324
  1699.9 424.9 %reduce-scatter.10.cloned.1.call-start = ((), (), s32[]{:S(2)}) async-start(), calls=%async_computation.12 | async-start | bytes 8650752 | tf_op jit(solution)/shard_map/reduce_scatter | solution.py:349
  1704.6 567.6 %reduce-scatter.6.cloned.1.call-start = ((), (), s32[]{:S(2)}) async-start(), calls=%async_computation.10 | async-start | bytes 8650752 | tf_op jit(solution)/shard_map/reduce_scatter | solution.py:347
  1709.3 772.1 %reduce-scatter.8.cloned.1.call-start = ((), (), s32[]{:S(2)}) async-start(), calls=%async_computation.11 | async-start | bytes 17842176 | tf_op jit(solution)/shard_map/reduce_scatter | solution.py:348
  1717.9 950.3 %reduce-scatter.12.cloned.1.call-start = ((), (), s32[]{:S(2)}) async-start(), calls=%async_computation.13 | async-start | bytes 17301504 | tf_op jit(solution)/shard_map/reduce_scatter | solution.py:350
  1727.5 1128.8 %reduce-scatter.14.cloned.1.call-start = ((), (), s32[]{:S(2)}) async-start(), calls=%async_computation.14 | async-start | bytes 17301504 | tf_op jit(solution)/shard_map/reduce_scatter | solution.py:351
  1740.7 1137.7 %copy-start.1 = (f32[128]{0:T(128)S(1)}, f32[128]{0:T(128)}, u32[]{:S(2)}) copy-start(f32[128]{0:T(128)} %param.47) | copy-start | bytes 1540
  (105 other events, 2920.9 us)
Sparse Core Ops, SparseCore 0:
  25.5 53.1 all-gather.18
  82.1 63.1 all-gather.10
  148.8 77.2 all-gather.8
  229.3 60.4 all-gather.12
  293.1 76.1 all-gather.14
  372.6 76.0 all-gather.16
  1699.0 151.2 all-reduce.9
  1858.2 126.1 all-reduce.11
  1987.4 137.3 reduce-scatter.9
  2127.6 144.5 reduce-scatter.5
  2280.3 201.0 reduce-scatter.7
  2484.2 183.9 reduce-scatter.11
  2671.2 185.0 reduce-scatter.13
where the time goes:
time: 2900 us; the launch traced here: 2890 us
  local copies, waits for them, and re-layouts  1110 us (38%)
  waiting for transfers between devices  1110 us (38%)
  other arithmetic  353 us (12%)
  matrix products  185 us (6%)
  blocking collectives  95.5 us (3%)
    reshape x16, local copies, waits for them, and re-layouts, toeplitz_rows(): return tiled.reshape(chans, block_len, 2 * block_len - 1)[:, :, :block_len]  370 us
    psum x2, waiting for transfers between devices, shards(): lax.psum((dnorm1_gain, dnorm1_bias, dvalue_bias, dema_delta, dema_alpha,...  238 us
    while x32, local copies, waits for them, and re-layouts  229 us
    reduce_scatter x1, waiting for transfers between devices, shards(): lax.psum_scatter(dbase_weight, ('seq', 'batch'), scatter_dimension=0, til...  209 us
    reduce_scatter x1, waiting for transfers between devices, shards(): lax.psum_scatter(dffn2_weight, ('seq', 'batch'), scatter_dimension=0, til...  188 us
    reduce_scatter x1, waiting for transfers between devices, shards(): lax.psum_scatter(dffn1_weight, ('seq', 'batch'), scatter_dimension=0, til...  187 us
    gather x1, local copies, waits for them, and re-layouts, rel_table(): return jnp.where(offsets >= 0, position_bias[jnp.maximum(offsets, 0)], 0.0)  168 us
    reduce_scatter x1, waiting for transfers between devices, shards(): lax.psum_scatter(dvalue_weight, ('seq', 'batch'), scatter_dimension=0, ti...  147 us
  transfers between devices with their start and end apart: 13, of which 7 were waited for; matrix products, arithmetic and copies ran while one was open for 29% of the time, Pallas kernels for 0%

commit v1 on v0

--- a/solution.py
+++ b/solution.py
@@ -1,6 +1,10 @@
+import functools
+
 import jax
 import jax.numpy as jnp
 from jax import lax
+from jax.experimental import pallas as pl
+from jax.experimental.pallas import tpu as pltpu
 from jax.sharding import PartitionSpec as P
 
 D = 1024
@@ -378,6 +382,1208 @@
     )
 
 
+VMEM_LIMIT = 63 * 1024 * 1024
+BF = jnp.bfloat16
+F32 = jnp.float32
+MESH = pl.DeviceIdType.MESH
+SCALE = ZD ** (-0.5)
+EMA_SCALE = NDIM ** (-0.5)
+BLK = 128
+VH = 1024
+BASE_COLS = 2176
+SM_ROWS = 400
+ROW_OMEGA, ROW_N1G, ROW_N1B, ROW_N2G, ROW_N2B = 256, 264, 272, 280, 288
+ROW_VB, ROW_BB, ROW_PB, ROW_F1B, ROW_F2B = 296, 312, 345, 353, 385
+ROW_SG, ROW_QO, ROW_POS = 393, 395, 396
+VALUE, BASE, PROJ, FFN1, FFN2 = range(5)
+U_V, U_P, U_BA, U_BB, U_1, U_2 = range(6)
+
+
+def pick(flag, yes, no):
+    return lax.select(flag, yes, no)
+
+
+def sig(v):
+    return jax.nn.sigmoid(v)
+
+
+def silu(v):
+    return v * sig(v)
+
+
+def slope(v):
+    s = sig(v)
+    return s * (1.0 + v * (1.0 - s))
+
+
+def dot_nn(a, b):
+    return jnp.dot(a, b, preferred_element_type=F32)
+
+
+def dot_nt(a, b):
+    return lax.dot_general(a, b, (((1,), (1,)), ((), ())), preferred_element_type=F32)
+
+
+def dot_tn(a, b):
+    return lax.dot_general(a, b, (((0,), (0,)), ((), ())), preferred_element_type=F32)
+
+
+def split_pair(first, second, low_lanes):
+    lo = jnp.where(low_lanes, first, pltpu.roll(second, 64, 1))
+    hi = jnp.where(low_lanes, pltpu.roll(first, 64, 1), second)
+    return lo, hi
+
+
+def fold8(v):
+    rows, cols = v.shape
+    return jnp.sum(v.reshape(rows // 8, 8, cols), axis=0)
+
+
+def shear(v, left):
+    rows = lax.broadcasted_iota(jnp.int32, (BLK, BLK), 0)
+    for bit in range(7):
+        step = 1 << bit
+        turned = pltpu.roll(v, BLK - step if left else step, 1)
+        v = jnp.where((rows & step) != 0, turned, v)
+    return v
+
+
+def layer_kernel(NS, *refs):
+    NZ = NS // 4
+    names = iter(refs)
+    take = lambda n: [next(names) for _ in range(n)]
+    (tok, og, n1g, n1b, vb, ema, om, bb, sg, qo, pbr, pbias, n2g, n2b, f1b, f2b) = take(16)
+    (vw, bw, pw, f1w, f2w) = take(5)
+    (o_block, o_tok, o_dv, o_db, o_dp, o_d1, o_d2, o_sm, o_ema) = take(9)
+    (WV, WB, WP, W1, W2) = take(5)
+    (G1, G2, GBA, GBB, RXBB) = take(5)
+    RY = take(6)
+    RZ = take(6)
+    (FV, FB, FXV, FXB, FX1) = take(5)
+    (SV, SB, NL, ML, NO, VP, VL, UH, UU, HH, SHP, RP, AD, GT, AT, PR, FO, FP, FG) = take(19)
+    (AS, AR, AX, AXR, OXR, GH, GUS, GBS, GA, GAT, GATR, GVP, GNVR) = take(13)
+    (XP, YP, GEP, GNP, HC, H8, EC, EXX, EXY, EXZ, BXX, BXY, BXZ, DEC, CIN, LAM, PIN) = take(17)
+    (SMR, SMX, SMY, SMZ, SMC) = take(5)
+    (in_sem, zs, zr, ys, yr, xs, xr, rxs, rxr, rys, ryr, rzs, rzr, es, er) = take(15)
+
+    s = lax.axis_index("seq")
+    b = lax.axis_index("batch")
+    x = lax.rem(s, 2)
+    y = lax.rem(lax.div(s, 2), 2)
+    z = lax.div(s, 4)
+    p = lax.div(s, 2)
+    q = 2 * x + b
+    xs_ = s + 1 - 2 * x
+    ys_ = s + 2 - 4 * y
+    C = (s, 1 - b)
+    X = (xs_, b)
+    XC = (xs_, 1 - b)
+    Y = (ys_, b)
+    ahead = lambda k: lax.rem(s + 4 * k, NS)
+    behind = lambda k: lax.rem(s - 4 * k + NS * 4, NS)
+    first = b == 0
+    al = pl.multiple_of
+    rows_of = lambda i, n: pl.ds(al(i * n, n), n)
+
+    loads = [
+        pltpu.make_async_copy(src, dst, in_sem.at[i])
+        for i, (src, dst) in enumerate(
+            ((vw, o_dv), (bw, o_db), (pw, o_dp), (f1w, o_d1), (f2w, o_d2))
+        )
+    ]
+    for load in loads:
+        load.start()
+
+    barrier = pltpu.get_barrier_semaphore()
+    partners = [C, X, XC, Y] + [(ahead(k), b) for k in range(1, NZ)]
+    for device in partners:
+        pl.semaphore_signal(barrier, inc=1, device_id=device, device_id_type=MESH)
+    pl.semaphore_wait(barrier, len(partners))
+
+    def remote(src, dst, send, recv, device):
+        return pltpu.make_async_remote_copy(
+            src_ref=src, dst_ref=dst, send_sem=send, recv_sem=recv, device_id=device, device_id_type=MESH
+        )
+
+    open_sends = []
+
+    def settle(copy):
+        open_sends[:] = [other for other in open_sends if other is not copy]
+
+    n_ex = [0]
+
+    def exchange(src, dst, device, landed=None):
+        i = n_ex[0]
+        n_ex[0] += 1
+        copy = remote(src, dst, es.at[i], er.at[i], device)
+        copy.start()
+        open_sends.append(copy)
+        arrival = copy if landed is None else remote(src, landed, es.at[i], er.at[i], device)
+        return copy, arrival
+
+    low1 = lambda n: lax.broadcasted_iota(jnp.int32, (n, BLK), 1) < 64
+
+    my_rows = pl.ds(al(64 * s + 32 * b, 32), 32)
+    other_rows = pl.ds(al(64 * s + 32 * (1 - b), 32), 32)
+
+    def split_columns(src, src0, blocks, mine_ref, mine_rows, dst0, other_ref):
+        low = low1(32)
+        for t in range(blocks):
+            lo, hi = split_pair(
+                src[:, src0 + 256 * t : src0 + 256 * t + 128],
+                src[:, src0 + 256 * t + 128 : src0 + 256 * t + 256],
+                low,
+            )
+            cols = slice(dst0 + 128 * t, dst0 + 128 * t + 128)
+            mine_ref[mine_rows, cols] = pick(first, lo, hi).astype(BF)
+            other_ref[:, cols] = pick(first, hi, lo).astype(BF)
+
+    loads[0].wait()
+    split_columns(o_dv, 0, 8, WV, my_rows, 0, SV)
+    _, got_wv = exchange(SV, WV.at[my_rows], C, WV.at[other_rows])
+    loads[1].wait()
+    WB[my_rows, 0:512] = o_db[:, pl.ds(al(512 * b, 512), 512)].astype(BF)
+    SB[:, 0:512] = o_db[:, pl.ds(al(512 * (1 - b), 512), 512)].astype(BF)
+    WB[my_rows, 512:1024] = o_db[:, pl.ds(al(3200 + 512 * b, 128), 512)].astype(BF)
+    SB[:, 512:1024] = o_db[:, pl.ds(al(3200 + 512 * (1 - b), 128), 512)].astype(BF)
+    shared_cols = o_db[:, 1024:1152].astype(BF)
+    WB[my_rows, 1024:1152] = shared_cols
+    SB[:, 1024:1152] = shared_cols
+    split_columns(o_db, 1152, 8, WB, my_rows, 1152, SB)
+    _, got_wb = exchange(SB, WB.at[my_rows], C, WB.at[other_rows])
+
+    gather = [WV, WB, WP, W1, W2]
+
+    def piece(w, chip):
+        if w < FFN1:
+            return gather[w].at[rows_of(chip, 64)]
+        return gather[w].at[rows_of(lax.div(chip, 2), 128)]
+
+    def send_z(w, k):
+        here = piece(w, s)
+        return remote(here, here, zs.at[w, k], zr.at[w, k], (ahead(k), b))
+
+    def got_z(w, k):
+        there = piece(w, behind(k))
+        return remote(there, there, zs.at[w, k], zr.at[w, k], (ahead(k), b))
+
+    def send_y(w, k):
+        part = piece(w, behind(k))
+        return remote(part, part, ys.at[w, k], yr.at[w, k], Y)
+
+    def got_y(w, k):
+        part = piece(w, ys_ + behind(k) - s)
+        return remote(part, part, ys.at[w, k], yr.at[w, k], Y)
+
+    def send_x(w, k, far):
+        chip = behind(k) if far == 0 else ys_ + behind(k) - s
+        part = piece(w, chip)
+        return remote(part, part, xs.at[w, far, k], xr.at[w, far, k], X)
+
+    def got_x(w, k, far):
+        chip = behind(k) if far == 0 else ys_ + behind(k) - s
+        part = piece(w, chip + xs_ - s)
+        return remote(part, part, xs.at[w, far, k], xr.at[w, far, k], X)
+
+    def open_gather(w):
+        for k in range(1, NZ):
+            send_z(w, k).start()
+        send_y(w, 0).start()
+        if w < FFN1:
+            send_x(w, 0, 0).start()
+
+    def relay_z(w):
+        def one(k, carry):
+            got_z(w, k).wait_recv()
+            send_y(w, k).start()
+            if w < FFN1:
+                send_x(w, k, 0).start()
+            return carry
+
+        lax.fori_loop(1, NZ, one, 0)
+
+    def relay_y(w):
+        def one(k, carry):
+            got_y(w, k).wait_recv()
+            if w < FFN1:
+                send_x(w, k, 1).start()
+            return carry
+
+        lax.fori_loop(0, NZ, one, 0)
+
+    def finish_x(w):
+        def one(k, carry):
+            got_x(w, k, 0).wait_recv()
+            got_x(w, k, 1).wait_recv()
+            return carry
+
+        lax.fori_loop(0, NZ, one, 0)
+
+    def close_gather(w):
+        def one(k, carry):
+            send_y(w, k).wait_send()
+            if w < FFN1:
+                send_x(w, k, 0).wait_send()
+                send_x(w, k, 1).wait_send()
+            return carry
+
+        lax.fori_loop(0, NZ, one, 0)
+
+        def plane(k, carry):
+            send_z(w, k).wait_send()
+            return carry
+
+        lax.fori_loop(1, NZ, plane, 0)
+
+    def norm_rows(v):
+        center = v - jnp.mean(v, axis=-1, keepdims=True)
+        rstd = lax.rsqrt(jnp.mean(center * center, axis=-1, keepdims=True) + 1e-05)
+        return center * rstd, rstd
+
+    own = rows_of(b, BLK)
+
+    def norm_one(i, carry):
+        rows = rows_of(i, 32)
+        n, _ = norm_rows(tok[rows, :].astype(F32))
+        normed = n * n1g[...] + n1b[...]
+        for g in range(8):
+            XP[pl.ds(al(128 * g + 32 * i, 32), 32), :] = normed[:, 128 * g : 128 * g + 128]
+        NL[pl.ds(al(128 * b + 32 * i, 32), 32), :] = normed.astype(BF)
+        return carry
+
+    got_wv.wait_recv()
+    open_gather(VALUE)
+    lax.fori_loop(0, 4, norm_one, 0)
+    _, got_nl = exchange(NL.at[own], NL.at[own], C, NL.at[rows_of(1 - b, BLK)])
+    got_wb.wait_recv()
+    open_gather(BASE)
+
+    NT = NO.at[0:512]
+    OG = NO.at[512:1024]
+    quad = lambda j: rows_of(j, BLK)
+
+    for j in range(NDIM):
+        rate = sig(ema[0, j])
+        DEC[j] = 1.0 - rate * sig(ema[1, j])
+        CIN[j] = rate * ema[2, j]
+        lam = DEC[j]
+        for _ in range(7):
+            lam = lam * lam
+        LAM[j] = lam
+
+    def panel(t):
+        return pl.ds(t, 8, stride=BLK)
+
+    def end_scan():
+        d = [DEC[j] for j in range(NDIM)]
+        c = [CIN[j] for j in range(NDIM)]
+
+        def step(t, h):
+            row = XP[panel(t), :]
+            return tuple(h[j] * d[j] + c[j] * row for j in range(NDIM))
+
+        h = lax.fori_loop(
+            0, BLK, step, tuple(jnp.zeros((8, 128), F32) for _ in range(NDIM)), unroll=4
+        )
+        for j in range(NDIM):
+            EC[0, j] = h[j]
+
+    end_scan()
+    _, got_ex = exchange(EC.at[0], EXX, X)
+
+    loads[2].wait()
+    WP[rows_of(s, 64), :] = o_dp[...].astype(BF)
+    loads[3].wait()
+    for j in range(4):
+        for t in range(8):
+            AS[32 * j : 32 * j + 32, 128 * t : 128 * t + 128] = o_d1[
+                :, 128 * (4 * t + j) : 128 * (4 * t + j) + 128
+            ].astype(BF)
+    f1_rows = lambda j: pl.ds(al(128 * p + 32 * j, 32), 32)
+    W1[f1_rows(q), :] = AS[rows_of(q, 32), :]
+    q_c = q + 1 - 2 * b
+    q_x = lax.rem(q + 2, 4)
+    q_xc = lax.rem(q_c + 2, 4)
+    f1_pairs = [
+        exchange(AS.at[rows_of(j, 32)], W1.at[f1_rows(q)], device, W1.at[f1_rows(j)])
+        for j, device in ((q_c, C), (q_x, X), (q_xc, XC))
+    ]
+    loads[4].wait()
+    W2[rows_of(p, 128), :] = o_d2[...].astype(BF)
+    OG[quad(q), :] = og[...]
+    copy_og_c, got_og_c = exchange(OG.at[quad(q)], OG.at[quad(q)], C, OG.at[quad(q_c)])
+    copy_og_x, got_og_x = exchange(OG.at[quad(q)], OG.at[quad(q)], X, OG.at[quad(q_x)])
+
+    open_gather(PROJ)
+    relay_z(VALUE)
+    relay_y(VALUE)
+
+    def scan_round_x(own_state, arrived, out, incoming, later):
+        for j in range(NDIM):
+            l, mine, theirs = LAM[j], own_state[j], arrived[j]
+            out[j] = pick(later, l * theirs + mine, l * mine + theirs)
+            incoming[j] = pick(later, theirs, jnp.zeros_like(theirs))
+
+    def scan_round_y(own_state, arrived, out, incoming, later, inner):
+        for j in range(NDIM):
+            l = LAM[j]
+            l2 = l * l
+            mine, theirs = own_state[j], arrived[j]
+            out[j] = pick(later, l2 * theirs + mine, l2 * mine + theirs)
+            hop = pick(inner == 1, l, jnp.ones_like(l))
+            incoming[j] += pick(later, hop * theirs, jnp.zeros_like(l))
+
+    def scan_round_z(arrived, incoming, reach, inner):
+        for j in range(NDIM):
+            l = LAM[j]
+            l2 = l * l
+            l4 = l2 * l2
+            one = jnp.ones_like(l)
+            hop = pick(lax.rem(inner, 2) == 1, l, one) * pick(inner >= 2, l2, one)
+            total = incoming[j]
+            for k in range(1, NZ):
+                total += pick(k <= reach, hop * arrived[k - 1, j], jnp.zeros_like(l))
+                hop = hop * l4
+            incoming[j] = total
+
+    got_ex.wait_recv()
+    scan_round_x(EC.at[0], EXX, EC.at[1], PIN, x == 1)
+    _, got_ey = exchange(EC.at[1], EXY, Y)
+    for copy, got in f1_pairs:
+        copy.wait_send()
+        settle(copy)
+        got.wait_recv()
+    open_gather(FFN1)
+    relay_z(BASE)
+    got_ey.wait_recv()
+    scan_round_y(EC.at[1], EXY, EC.at[2], PIN, y == 1, x)
+    got_ez = [exchange(EC.at[2], EXZ.at[k - 1], (ahead(k), b))[1] for k in range(1, NZ)]
+    open_gather(FFN2)
+    relay_y(BASE)
+    got_og_x.wait_recv()
+    copy_og_xc, got_og_xc = exchange(OG.at[quad(q_x)], OG.at[quad(q_x)], C, OG.at[quad(q_xc)])
+    relay_z(PROJ)
+    relay_y(PROJ)
+    for got in got_ez:
+        got.wait_recv()
+    scan_round_z(EXZ, PIN, z, 2 * y + x)
+
+    def forward_scan():
+        for half in range(2):
+            js = range(8 * half, 8 * half + 8)
+            d = [DEC[j] for j in js]
+            c = [CIN[j] for j in js]
+            g = [EMA_SCALE * ema[3, j] for j in js]
+
+            def group(i, h):
+                for n, j in enumerate(js):
+                    HC[i, j] = h[n]
+                for u in range(8):
+                    t = 8 * i + u
+                    row = XP[panel(t), :]
+                    h = tuple(h[n] * d[n] + c[n] * row for n in range(8))
+                    out = g[0] * h[0]
+                    for n in range(1, 8):
+                        out = out + g[n] * h[n]
+                    if half == 0:
+                        out = out + om[...] * row
+                    else:
+                        out = out + YP[panel(t), :]
+                    YP[panel(t), :] = out
+                return h
+
+            lax.fori_loop(0, 16, group, tuple(PIN[j] for j in js))
+
+    forward_scan()
+
+    def mixed_one(i, carry):
+        for g in range(8):
+            v = YP[pl.ds(al(128 * g + 32 * i, 32), 32), :]
+            ML[pl.ds(al(128 * b + 32 * i, 32), 32), 128 * g : 128 * g + 128] = silu(v).astype(BF)
+        return carry
+
+    lax.fori_loop(0, 4, mixed_one, 0)
+    _, got_ml = exchange(ML.at[own], ML.at[own], C, ML.at[rows_of(1 - b, BLK)])
+
+    low_row = low1(1)
+
+    def my_half(ref, start):
+        parts = []
+        for t in range(8):
+            lo, hi = split_pair(
+                ref[:, start + 256 * t : start + 256 * t + 128],
+                ref[:, start + 256 * t + 128 : start + 256 * t + 256],
+                low_row,
+            )
+            parts.append(pick(first, lo, hi))
+        return jnp.concatenate(parts, axis=1)
+
+    got_nl.wait_recv()
+    finish_x(VALUE)
+    vbias = my_half(vb, 0)
+    for n in range(2):
+        cols = slice(512 * n, 512 * n + 512)
+        v = dot_nn(NL[...], WV[:, cols]) + vbias[:, cols]
+        VP[:, cols] = v.astype(BF)
+        VL[:, cols] = silu(v).astype(BF)
+
+    relay_z(FFN1)
+
+    got_ml.wait_recv()
+    finish_x(BASE)
+    UH[:, 0:512] = dot_nn(ML[...], WB[:, 0:512]) + bb[:, pl.ds(al(512 * b, 512), 512)]
+    UH[:, 512:1024] = dot_nn(ML[...], WB[:, 512:1024]) + bb[:, pl.ds(al(3200 + 512 * b, 128), 512)]
+    theirs = rows_of(1 - b, BLK)
+    my_cols = pl.ds(al(512 * b, 512), 512)
+    their_cols = pl.ds(al(512 * (1 - b), 512), 512)
+    copy_u, got_u = exchange(UH.at[theirs, 0:512], UU.at[:, my_cols], C, UU.at[:, their_cols])
+    copy_h, got_h = exchange(UH.at[theirs, 512:1024], HH.at[:, my_cols], C, HH.at[:, their_cols])
+    UU[:, my_cols] = UH[own, 0:512]
+    HH[:, my_cols] = UH[own, 512:1024]
+    SHP[...] = dot_nn(ML[...], WB[:, 1024:1152]) + bb[:, 1024:1152]
+    rbias = my_half(bb, 1152)
+    for n in range(2):
+        RP[:, 512 * n : 512 * n + 512] = (
+            dot_nn(ML[...], WB[:, 1152 + 512 * n : 1664 + 512 * n]) + rbias[:, 512 * n : 512 * n + 512]
+        ).astype(BF)
+
+    shared_of = lambda i: silu(SHP[128 * i : 128 * i + 128, :])
+
+    def queries_keys(i):
+        sh = shared_of(i)
+        return (sh * sg[0:1, :] + qo[...]).astype(BF), (sh * sg[1:2, :]).astype(BF)
+
+    position = shear(jnp.broadcast_to(pbr[...], (BLK, BLK)), False)
+    at_row = lax.broadcasted_iota(jnp.int32, (BLK, BLK), 0)
+    at_col = lax.broadcasted_iota(jnp.int32, (BLK, BLK), 1)
+    causal = at_row >= at_col
+    for i in range(2):
+        rows = slice(128 * i, 128 * i + 128)
+        qs, ks = queries_keys(i)
+        scores = jnp.where(causal, dot_nt(qs, ks) * SCALE + position, -jnp.inf)
+        e = jnp.exp(scores - jnp.max(scores, axis=-1, keepdims=True))
+        attn = e / jnp.sum(e, axis=-1, keepdims=True)
+        AT[rows, :] = attn
+        low = attn.astype(BF)
+        for n in range(2):
+            cols = slice(512 * n, 512 * n + 512)
+            att = dot_nn(low, VL[rows, cols])
+            AD[rows, cols] = att.astype(BF)
+            GT[rows, cols] = (att * silu(RP[rows, cols].astype(F32))).astype(BF)
+
+    relay_z(FFN2)
+
+    finish_x(PROJ)
+    copy_u.wait_send()
+    copy_h.wait_send()
+    settle(copy_u)
+    settle(copy_h)
+    for n in range(2):
+        cols = slice(512 * n, 512 * n + 512)
+        UH[:, cols] = dot_nn(GT[...], WP[:, cols])
+    copy_p, got_p = exchange(UH.at[theirs], PR, C)
+    got_u.wait_recv()
+    got_h.wait_recv()
+    got_p.wait_recv()
+
+    def residual_one(i, carry):
+        rows = rows_of(i, 32)
+        mine = pl.ds(al(128 * b + 32 * i, 32), 32)
+        total = HH[rows, :] + ((UH[mine, :] + PR[rows, :]) + pbias[...])
+        HH[rows, :] = total
+        base = tok[rows, :].astype(F32)
+        out = base + sig(UU[rows, :]) * (silu(total) - base)
+        FO[rows, :] = out
+        n, _ = norm_rows(out)
+        NT[pl.ds(al(128 * q + 32 * i, 32), 32), :] = (n * n2g[...] + n2b[...]).astype(BF)
+        return carry
+
+    lax.fori_loop(0, 4, residual_one, 0)
+    copy_nt_x, got_nt_x = exchange(NT.at[quad(q)], NT.at[quad(q)], X, NT.at[quad(q_x)])
+    copy_nt_c, got_nt_c = exchange(NT.at[quad(q)], NT.at[quad(q)], C, NT.at[quad(q_c)])
+
+    relay_y(FFN1)
+    relay_y(FFN2)
+    got_og_c.wait_recv()
+    got_og_xc.wait_recv()
+    for m in range(2):
+        for n in range(2):
+            rows = slice(256 * m, 256 * m + 256)
+            cols = slice(512 * n, 512 * n + 512)
+            FP[rows, cols] = dot_nt(OG[rows, :], W2[cols, :])
+    got_nt_x.wait_recv()
+    copy_nt_xc, got_nt_xc = exchange(NT.at[quad(q_x)], NT.at[quad(q_x)], C, NT.at[quad(q_xc)])
+    got_nt_c.wait_recv()
+    got_nt_xc.wait_recv()
+
+    FL = FG.at[0:512]
+    GF = FG.at[512:1024]
+    fbias = jnp.concatenate(
+        [f1b[:, pl.ds(al(512 * t + 128 * q, 128), 128)] for t in range(8)], axis=1
+    )
+    for m in range(2):
+        for n in range(2):
+            rows = slice(256 * m, 256 * m + 256)
+            cols = slice(512 * n, 512 * n + 512)
+            pre = dot_nn(NT[rows, :], W1[:, cols]) + fbias[:, cols]
+            FL[rows, cols] = silu(pre).astype(BF)
+            GF[rows, cols] = (FP[rows, cols] * slope(pre)).astype(BF)
+    for m in range(2):
+        for n in range(2):
+            rows = slice(256 * m, 256 * m + 256)
+            cols = slice(512 * n, 512 * n + 512)
+            AS[rows, cols] = dot_nt(GF[rows, :], W1[cols, :]).astype(BF)
+
+    def reduce_pair(staged, landing):
+        copies = []
+        for c in range(2):
+            there = rows_of(2 * c + 1 - b, BLK)
+            copies.append(exchange(staged.at[there], landing.at[rows_of(c, BLK)], C))
+        return copies
+
+    def reduce_x(staged, landing, arrivals, out, out_landing):
+        for _, arrival in arrivals:
+            arrival.wait_recv()
+
+        def one(i, carry):
+            mine = pl.ds(al(128 * (2 * (1 - x) + b) + 32 * i, 32), 32)
+            got = pl.ds(al(128 * (1 - x) + 32 * i, 32), 32)
+            out[rows_of(i, 32), :] = (staged[mine, :].astype(F32) + landing[got, :].astype(F32)).astype(BF)
+            return carry
+
+        lax.fori_loop(0, 4, one, 0)
+        return exchange(out, out_landing, X)
+
+    def reduced(staged, landing, out_landing, i):
+        mine = pl.ds(al(128 * q + 32 * i, 32), 32)
+        got = pl.ds(al(128 * x + 32 * i, 32), 32)
+        return (
+            staged[mine, :].astype(F32)
+            + landing[got, :].astype(F32)
+            + out_landing[rows_of(i, 32), :].astype(F32)
+        )
+
+    got_a = reduce_pair(AS, AR)
+
+    def store_row(row, v):
+        for g in range(v.shape[1] // 128):
+            SM_OUT[row + g : row + g + 1, :] = v[:, 128 * g : 128 * g + 128]
+
+    SM_OUT = o_sm
+    SM_OUT[...] = jnp.zeros((SM_ROWS, 128), F32)
+
+    def weight_grad(left, right, out, right0, out0, width):
+        tile = 512 if width % 512 == 0 else 384
+        for m in range(2):
+            for n in range(width // tile):
+                out[512 * m : 512 * m + 512, out0 + tile * n : out0 + tile * n + tile] = dot_tn(
+                    left[:, 512 * m : 512 * m + 512],
+                    right[:, right0 + tile * n : right0 + tile * n + tile],
+                ).astype(BF)
+
+    grads = [NO, FG, GBA, GBB, G1, G2]
+    RXV = W1.at[0:512]
+    RXP = W1.at[512:1024]
+    RXBA = W2.at[0:512]
+    half = [RXV, RXP, RXBA, RXBB]
+
+    def shard(u, chip):
+        if u < U_1:
+            return rows_of(chip, 64)
+        return rows_of(lax.div(chip, 2), 128)
+
+    def rs_x(u, k, far):
+        plane = ahead(k)
+        chip = plane if far == 0 else plane + ys_ - s
+        src = grads[u].at[shard(u, chip + xs_ - s)]
+        slot = half[u].at[pl.ds(al(64 * (2 * k + far), 64), 64)]
+        return remote(src, slot, rxs.at[u, k, far], rxr.at[u, k, far], X)
+
+    def rs_y(u, k):
+        src = grads[u].at[shard(u, ahead(k) + ys_ - s)]
+        return remote(src, RY[u].at[k], rys.at[u, k], ryr.at[u, k], Y)
+
+    def rs_z(u, k):
+        src = grads[u].at[shard(u, ahead(k))]
+        return remote(src, RZ[u].at[k - 1], rzs.at[u, k], rzr.at[u, k], (ahead(k), b))
+
+    turn = lambda i: lax.rem(i + 1, NZ)
+
+    def rs_open(u):
+        def one(i, carry):
+            k = turn(i)
+            if u < U_1:
+                rs_x(u, k, 1).start()
+                rs_x(u, k, 0).start()
+            else:
+                rs_y(u, k).start()
+            return carry
+
+        lax.fori_loop(0, NZ, one, 0)
+
+    def rs_pass_x(u):
+        def one(i, carry):
+            k = turn(i)
+            plane = ahead(k)
+            for far in (1, 0):
+                rs_x(u, k, far).wait_recv()
+                chip = plane if far == 0 else plane + ys_ - s
+                rows = shard(u, chip)
+                got = half[u][pl.ds(al(64 * (2 * k + far), 64), 64), :]
+                grads[u][rows, :] = (grads[u][rows, :].astype(F32) + got.astype(F32)).astype(BF)
+                if far == 1:
+                    rs_y(u, k).start()
+            return carry
+
+        lax.fori_loop(0, NZ, one, 0)
+
+    def rs_pass_y(u):
+        def one(i, carry):
+            k = i + 1
+            rs_y(u, k).wait_recv()
+            rows = shard(u, ahead(k))
+            grads[u][rows, :] = (grads[u][rows, :].astype(F32) + RY[u][k].astype(F32)).astype(BF)
+            rs_z(u, k).start()
+            return carry
+
+        lax.fori_loop(0, NZ - 1, one, 0)
+        rs_y(u, 0).wait_recv()
+
+    def rs_total(u, rows_in):
+        rows = shard(u, s)
+        size = 64 if u < U_1 else 128
+        start = size * (s if u < U_1 else p)
+        at = pl.ds(al(start + rows_in[0], 16), rows_in[1])
+        in_ = pl.ds(al(rows_in[0], 16), rows_in[1])
+        total = grads[u][at, :].astype(F32) + RY[u][0, in_, :].astype(F32)
+        for k in range(1, NZ):
+            total += RZ[u][k - 1, in_, :].astype(F32)
+        return total
+
+    def rs_wait_z(u):
+        def one(k, carry):
+            rs_z(u, k).wait_recv()
+            return carry
+
+        lax.fori_loop(1, NZ, one, 0)
+
+    def column_sum(ref, start, width):
+        def one(i, acc):
+            return acc + fold8(ref[rows_of(i, 32), start : start + width].astype(F32))
+
+        acc = lax.fori_loop(0, ref.shape[0] // 32, one, jnp.zeros((8, width), F32))
+        return jnp.sum(acc, axis=0, keepdims=True)
+
+    weight_grad(FL, OG, G2, 0, 0, 1024)
+    rs_open(U_2)
+    a_x = reduce_x(AS, AR, got_a, AX, AXR)
+    weight_grad(NT, GF, G1, 0, 0, 1024)
+    rs_open(U_1)
+    f1_sum = column_sum(GF, 0, 1024)
+    for t in range(8):
+        SM_OUT[pl.ds(ROW_F1B + 4 * t + q, 1), :] = f1_sum[:, 128 * t : 128 * t + 128]
+
+    a_x[1].wait_recv()
+
+    def back_two(i, carry):
+        rows = rows_of(i, 32)
+        a = reduced(AS, AR, AXR, i)
+        n, rstd = norm_rows(FO[rows, :])
+        g = a * n2g[...]
+        grad = og[rows, :].astype(F32) + (
+            g - jnp.mean(g, axis=-1, keepdims=True) - n * jnp.mean(g * n, axis=-1, keepdims=True)
+        ) * rstd
+        update = sig(UU[rows, :])
+        total = HH[rows, :]
+        logistic = sig(total)
+        base = tok[rows, :].astype(F32)
+        gh = (grad * update * (logistic * (1.0 + total * (1.0 - logistic)))).astype(BF)
+        GH[pl.ds(al(128 * b + 32 * i, 32), 32), :] = gh
+        GUS[rows, :] = (grad * (total * logistic - base) * update * (1.0 - update)).astype(BF)
+        PR[rows, :] = grad * (1.0 - update)
+        return (
+            carry[0] + fold8(a * n),
+            carry[1] + fold8(a),
+            carry[2] + fold8(gh.astype(F32)),
+            carry[3] + fold8(og[rows, :].astype(F32)),
+        )
+
+    zero8 = jnp.zeros((8, 1024), F32)
+    sums = lax.fori_loop(0, 4, back_two, (zero8, zero8, zero8, zero8))
+    _, got_gh = exchange(GH.at[own], GH.at[own], C, GH.at[theirs])
+    _, got_gu = exchange(GUS.at[:, their_cols], GBS.at[own, 0:512], C, GBS.at[theirs, 0:512])
+    GBS[own, 0:512] = GUS[:, my_cols]
+    for row, acc in zip((ROW_N2G, ROW_N2B, ROW_PB, ROW_F2B), sums):
+        store_row(row, jnp.sum(acc, axis=0, keepdims=True))
+
+    got_gh.wait_recv()
+    for copy, _ in got_a:
+        copy.wait_send()
+        settle(copy)
+    for m in range(2):
+        for n in range(2):
+            rows = slice(256 * m, 256 * m + 256)
+            cols = slice(512 * n, 512 * n + 512)
+            AS[rows, cols] = dot_nn(FL[rows, :], W2[:, cols]).astype(BF)
+    got_o = reduce_pair(AS, AR)
+    close_gather(FFN1)
+    close_gather(FFN2)
+
+    for n in range(2):
+        cols = slice(512 * n, 512 * n + 512)
+        gg = dot_nt(GH[...], WP[cols, :])
+        pre = RP[:, cols].astype(F32)
+        logistic = sig(pre)
+        GA[:, cols] = (gg * (pre * logistic)).astype(BF)
+        GBS[:, 1152 + 512 * n : 1664 + 512 * n] = (
+            gg * AD[:, cols].astype(F32) * (logistic * (1.0 + pre * (1.0 - logistic)))
+        ).astype(BF)
+    for i in range(2):
+        rows = slice(128 * i, 128 * i + 128)
+        GAT[rows, :] = dot_nt(GA[rows, :], VL[rows, :])
+    _, got_gat = exchange(GAT, GATR, C)
+    a_x[0].wait_send()
+    settle(a_x[0])
+    o_x = reduce_x(AS, AR, got_o, AX, OXR)
+    for i in range(2):
+        rows = slice(128 * i, 128 * i + 128)
+        low = AT[rows, :].astype(BF)
+        for n in range(2):
+            cols = slice(512 * n, 512 * n + 512)
+            gv = dot_tn(low, GA[rows, cols])
+            GVP[rows, cols] = (gv * slope(VP[rows, cols].astype(F32))).astype(BF)
+    GBS[:, 512:1024] = GH[:, my_cols]
+    o_x[1].wait_recv()
+    weight_grad(GT, GH, FG, 0, 0, 1024)
+    rs_open(U_P)
+    got_gat.wait_recv()
+    for i in range(2):
+        rows = slice(128 * i, 128 * i + 128)
+        attn = AT[rows, :]
+        gat = GAT[rows, :] + GATR[rows, :]
+        gs = (attn * (gat - jnp.sum(gat * attn, axis=-1, keepdims=True))).astype(BF)
+        qs, ks = queries_keys(i)
+        gq = dot_nn(gs, ks) * SCALE
+        gk = dot_tn(gs, qs) * SCALE
+        pre = SHP[rows, :]
+        sh = silu(pre)
+        GBS[rows, 1024:1152] = ((gq * sg[0:1, :] + gk * sg[1:2, :]) * slope(pre)).astype(BF)
+        mine = b == i
+
+        @pl.when(mine)
+        def _(gs=gs, gq=gq, gk=gk, sh=sh):
+            SM_OUT[ROW_SG : ROW_SG + 1, :] = jnp.sum(gq * sh, axis=0, keepdims=True)
+            SM_OUT[ROW_SG + 1 : ROW_SG + 2, :] = jnp.sum(gk * sh, axis=0, keepdims=True)
+            SM_OUT[ROW_QO : ROW_QO + 1, :] = jnp.sum(gq, axis=0, keepdims=True)
+            SM_OUT[ROW_POS : ROW_POS + 1, :] = jnp.sum(
+                shear(gs.astype(F32), True), axis=0, keepdims=True
+            )
+
+    got_gu.wait_recv()
+    weight_grad(ML, GBS, GBA, 0, 0, 1024)
+    rs_open(U_BA)
+    weight_grad(ML, GBS, GBB, 1024, 0, 1152)
+    rs_open(U_BB)
+    base_sum = column_sum(GBS, 0, BASE_COLS)
+    for t in range(4):
+        cols = slice(128 * t, 128 * t + 128)
+        SM_OUT[pl.ds(ROW_BB + 4 * b + t, 1), :] = base_sum[:, cols]
+        SM_OUT[pl.ds(ROW_BB + 25 + 4 * b + t, 1), :] = base_sum[:, 512 + 128 * t : 640 + 128 * t]
+    SM_OUT[ROW_BB + 8 : ROW_BB + 9, :] = base_sum[:, 1024:1152] * 0.5
+
+    low_float = low_row.astype(F32)
+    keep = pick(first, low_float, 1.0 - low_float)
+
+    def store_half(row, v):
+        for t in range(8):
+            block = v[:, 128 * t : 128 * t + 128]
+            turned = pltpu.roll(block, 64, 1)
+            SM_OUT[row + 2 * t : row + 2 * t + 1, :] = keep * pick(first, block, turned)
+            SM_OUT[row + 2 * t + 1 : row + 2 * t + 2, :] = keep * pick(first, turned, block)
+
+    store_half(ROW_BB + 9, base_sum[:, 1152:2176])
+    GBS[:, 1024:1152] = (GBS[:, 1024:1152].astype(F32) * 0.5).astype(BF)
+    GM = FP.at[0:256]
+    GNV = FP.at[256:512]
+    for n in range(2):
+        cols = slice(512 * n, 512 * n + 512)
+        GM[:, cols] = dot_nt(GBS[...], WB[cols, :])
+    _, got_gm = exchange(GM.at[theirs], GNVR.at[0], C)
+    for n in range(2):
+        cols = slice(512 * n, 512 * n + 512)
+        GNV[:, cols] = dot_nt(GVP[...], WV[cols, :])
+    _, got_gnv = exchange(GNV.at[theirs], GNVR.at[1], C)
+    for copy in (copy_og_c, copy_og_x, copy_og_xc, copy_nt_x, copy_nt_c, copy_nt_xc):
+        copy.wait_send()
+        settle(copy)
+    weight_grad(NL, GVP, NO, 0, 0, 1024)
+    rs_open(U_V)
+    store_half(ROW_VB, column_sum(GVP, 0, 1024))
+
+    got_gm.wait_recv()
+
+    def grad_ema_one(i, carry):
+        for g in range(8):
+            cols = slice(128 * g, 128 * g + 128)
+            rows = pl.ds(al(128 * g + 32 * i, 32), 32)
+            v = GM[pl.ds(al(128 * b + 32 * i, 32), 32), cols] + GNVR[0, rows_of(i, 32), cols]
+            GEP[rows, :] = v * slope(YP[rows, :])
+        return carry
+
+    lax.fori_loop(0, 4, grad_ema_one, 0)
+
+    def adjoint_end():
+        d = [DEC[j] for j in range(NDIM)]
+
+        def step(i, g):
+            row = GEP[panel(BLK - 1 - i), :]
+            return tuple(g[j] * d[j] + row for j in range(NDIM))
+
+        g = lax.fori_loop(
+            0, BLK, step, tuple(jnp.zeros((8, 128), F32) for _ in range(NDIM)), unroll=4
+        )
+        for j in range(NDIM):
+            EC[3, j] = g[j]
+
+    adjoint_end()
+    _, got_bx = exchange(EC.at[3], BXX, X)
+    rs_pass_y(U_2)
+    got_bx.wait_recv()
+    scan_round_x(EC.at[3], BXX, EC.at[4], PIN, x == 0)
+    _, got_by = exchange(EC.at[4], BXY, Y)
+    rs_pass_y(U_1)
+    got_by.wait_recv()
+    scan_round_y(EC.at[4], BXY, EC.at[5], PIN, y == 0, 1 - x)
+    got_bz = [
+        exchange(EC.at[5], BXZ.at[k - 1], (ahead(NZ - k), b))[1] for k in range(1, NZ)
+    ]
+    rs_pass_x(U_P)
+
+    def block_out_one(i, carry):
+        rows = rows_of(i, 32)
+        o_block[rows, :] = (FO[rows, :] + (reduced(AS, AR, OXR, i) + f2b[...])).astype(BF)
+        return carry
+
+    lax.fori_loop(0, 4, block_out_one, 0)
+    for got in got_bz:
+        got.wait_recv()
+    scan_round_z(BXZ, PIN, NZ - 1 - z, 2 * (1 - y) + 1 - x)
+
+    def backward_scan():
+        for part in range(2):
+            js = range(8 * part, 8 * part + 8)
+            d = [DEC[j] for j in js]
+            c = [CIN[j] for j in js]
+            e = [EMA_SCALE * CIN[j] * ema[3, j] for j in js]
+
+            def group(i, carry):
+                at = 15 - i
+                h = tuple(HC[at, j] for j in js)
+                for u in range(8):
+                    for n in range(8):
+                        H8[u, n] = h[n]
+                    if u < 7:
+                        row = XP[panel(8 * at + u), :]
+                        h = tuple(h[n] * d[n] + c[n] * row for n in range(8))
+                g, s1, m = carry
+                for u in range(7, -1, -1):
+                    t = 8 * at + u
+                    row = XP[panel(t), :]
+                    ge = GEP[panel(t), :]
+                    g = tuple(g[n] * d[n] + ge for n in range(8))
+                    s1 = tuple(s1[n] + row * g[n] for n in range(8))
+                    m = tuple(m[n] + g[n] * H8[u, n] for n in range(8))
+                    out = e[0] * g[0]
+                    for n in range(1, 8):
+                        out = out + e[n] * g[n]
+                    if part == 0:
+                        out = out + om[...] * ge
+                    else:
+                        out = out + GNP[panel(t), :]
+                    GNP[panel(t), :] = out
+                return g, s1, m
+
+            zeros = tuple(jnp.zeros((8, 128), F32) for _ in range(8))
+            _, s1, m = lax.fori_loop(0, 16, group, (tuple(PIN[j] for j in js), zeros, zeros))
+            for n, j in enumerate(js):
+                SM_OUT[8 * j : 8 * j + 8, :] = s1[n]
+                SM_OUT[128 + 8 * j : 128 + 8 * j + 8, :] = m[n]
+
+    backward_scan()
+
+    for g in range(8):
+        rows = slice(128 * g, 128 * g + 128)
+        SM_OUT[ROW_OMEGA + g : ROW_OMEGA + g + 1, :] = jnp.sum(
+            fold8(XP[rows, :] * GEP[rows, :]), axis=0, keepdims=True
+        )
+
+    got_gnv.wait_recv()
+
+    def back_one(i, carry):
+        rows = rows_of(i, 32)
+        wide = jnp.concatenate(
+            [GNP[pl.ds(al(128 * g + 32 * i, 32), 32), :] for g in range(8)], axis=1
+        )
+        a = (GNV[pl.ds(al(128 * b + 32 * i, 32), 32), :] + GNVR[1, rows, :]) + wide
+        n, rstd = norm_rows(tok[rows, :].astype(F32))
+        g = a * n1g[...]
+        back = (
+            g - jnp.mean(g, axis=-1, keepdims=True) - n * jnp.mean(g * n, axis=-1, keepdims=True)
+        ) * rstd
+        o_tok[rows, :] = (PR[rows, :] + back).astype(BF)
+        return carry[0] + fold8(a * n), carry[1] + fold8(a)
+
+    sums = lax.fori_loop(0, 4, back_one, (zero8, zero8))
+    for row, acc in zip((ROW_N1G, ROW_N1B), sums):
+        store_row(row, jnp.sum(acc, axis=0, keepdims=True))
+
+    half_rows = SM_ROWS // 2
+    my_part = rows_of(b, half_rows)
+    their_part = rows_of(1 - b, half_rows)
+    copy_c, got_c = exchange(SM_OUT.at[their_part], SMR, C)
+    rs_pass_x(U_BA)
+    got_c.wait_recv()
+    SMX[0] = SM_OUT[my_part, :] + SMR[...]
+    _, got_sx = exchange(SMX.at[0], SMX.at[1], X)
+    rs_pass_y(U_P)
+    got_sx.wait_recv()
+    SMY[0] = SMX[0] + SMX[1]
+    _, got_sy = exchange(SMY.at[0], SMY.at[1], Y)
+    rs_pass_y(U_BA)
+    got_sy.wait_recv()
+    SMZ[0] = SMY[0] + SMY[1]
+    got_sz = [exchange(SMZ.at[0], SMZ.at[k], (ahead(k), b))[1] for k in range(1, NZ)]
+    rs_pass_x(U_BB)
+    rs_pass_x(U_V)
+    for got in got_sz:
+        got.wait_recv()
+    total = SMZ[lax.rem(z, NZ)]
+    for k in range(1, NZ):
+        total = total + SMZ[lax.rem(z + NZ - k, NZ)]
+    SM_OUT[my_part, :] = total
+    _, got_cc = exchange(SM_OUT.at[my_part], SMC, C)
+
+    rs_pass_y(U_BB)
+    rs_pass_y(U_V)
+    rs_wait_z(U_2)
+    for i in range(4):
+        o_d2[32 * i : 32 * i + 32, :] = rs_total(U_2, (32 * i, 32))
+    rs_wait_z(U_1)
+    for i in range(4):
+        o_d1[:, 1024 * i : 1024 * i + 1024] = rs_total(U_1, (32 * i, 32))
+    quarter = lambda j: pl.ds(al(1024 * j, 1024), 1024)
+    d1_pairs = [
+        exchange(o_d1.at[:, quarter(j)], FX1.at[q], device, FX1.at[j])
+        for j, device in ((q_c, C), (q_x, X), (q_xc, XC))
+    ]
+    rs_wait_z(U_P)
+    for i in range(2):
+        o_dp[32 * i : 32 * i + 32, :] = rs_total(U_P, (32 * i, 32))
+    mine32 = 32 * b
+    their32 = 32 * (1 - b)
+    h_mine = pl.ds(al(3200 + 512 * b, 128), 512)
+    h_their = pl.ds(al(3200 + 512 * (1 - b), 128), 512)
+    low = low1(32)
+
+    def merge(out, start, own_half, other_half):
+        for t in range(8):
+            cols = slice(128 * t, 128 * t + 128)
+            m, o = own_half[:, cols], other_half[:, cols]
+            lo, hi = pick(first, m, o), pick(first, o, m)
+            at = start + 256 * t
+            out[:, at : at + 128] = jnp.where(low, lo, pltpu.roll(hi, 64, 1))
+            out[:, at + 128 : at + 256] = jnp.where(low, pltpu.roll(lo, 64, 1), hi)
+
+    rs_wait_z(U_BA)
+    FB[:, 0:1024] = rs_total(U_BA, (their32, 32))
+    _, got_ba = exchange(FB.at[:, 0:1024], FXB.at[:, 0:1024], C)
+    part = rs_total(U_BA, (mine32, 32))
+    o_db[:, my_cols] = part[:, 0:512]
+    o_db[:, h_mine] = part[:, 512:1024]
+    rs_wait_z(U_BB)
+    FB[:, 1024:2176] = rs_total(U_BB, (their32, 32))
+    _, got_bb = exchange(FB.at[:, 1024:2176], FXB.at[:, 1024:2176], C)
+    part = rs_total(U_BB, (mine32, 32))
+    o_db[:, 1024:1152] = part[:, 0:128]
+    rs_wait_z(U_V)
+    FV[...] = rs_total(U_V, (their32, 32))
+    _, got_v = exchange(FV, FXV, C)
+    part_v = rs_total(U_V, (mine32, 32))
+
+    FX1[q] = o_d1[:, quarter(q)]
+    for copy, got in d1_pairs:
+        copy.wait_send()
+        settle(copy)
+        got.wait_recv()
+    for j in range(4):
+        for t in range(8):
+            o_d1[:, 128 * (4 * t + j) : 128 * (4 * t + j) + 128] = FX1[j, :, 128 * t : 128 * t + 128]
+
+    copy_c.wait_send()
+    settle(copy_c)
+    got_cc.wait_recv()
+    SM_OUT[their_part, :] = SMC[...]
+    for j in range(NDIM):
+        rate, damping = sig(ema[0, j]), sig(ema[1, j])
+        beta, gamma = ema[2, j], EMA_SCALE * ema[3, j]
+        s1 = SM_OUT[8 * j : 8 * j + 8, :]
+        m = gamma * SM_OUT[128 + 8 * j : 136 + 8 * j, :]
+        o_ema[0, j] = (beta * gamma * s1 - damping * m) * rate * (1.0 - rate)
+        o_ema[1, j] = -rate * m * damping * (1.0 - damping)
+        o_ema[2, j] = gamma * rate * s1
+        o_ema[3, j] = EMA_SCALE * rate * beta * s1
+
+    got_ba.wait_recv()
+    o_db[:, their_cols] = FXB[:, 0:512]
+    o_db[:, h_their] = FXB[:, 512:1024]
+    got_bb.wait_recv()
+    merge(o_db, 1152, part[:, 128:1152], FXB[:, 1152:2176])
+    got_v.wait_recv()
+    merge(o_dv, 0, part_v, FXV[...])
+
+    for copy in open_sends:
+        copy.wait_send()
+    for w in (VALUE, BASE, PROJ):
+        close_gather(w)
+
+    def close_sums(u):
+        def one(k, carry):
+            rs_y(u, k).wait_send()
+            if u < U_1:
+                rs_x(u, k, 0).wait_send()
+                rs_x(u, k, 1).wait_send()
+            return carry
+
+        lax.fori_loop(0, NZ, one, 0)
+
+        def plane(k, carry):
+            rs_z(u, k).wait_send()
+            return carry
+
+        lax.fori_loop(1, NZ, plane, 0)
+
+    for u in (U_V, U_P, U_BA, U_BB, U_1, U_2):
+        close_sums(u)
+
+
+def fast_shards(
+    tokens,
+    out_grad,
+    norm1_gain,
+    norm1_bias,
+    value_weight,
+    value_bias,
+    ema_delta,
+    ema_alpha,
+    ema_beta,
+    ema_gamma,
+    ema_omega,
+    base_weight,
+    base_bias,
+    shared_gamma,
+    query_offset,
+    position_bias,
+    proj_weight,
+    proj_bias,
+    norm2_gain,
+    norm2_bias,
+    ffn1_weight,
+    ffn1_bias,
+    ffn2_weight,
+    ffn2_bias,
+):
+    NS = lax.axis_size("seq")
+    NZ = NS // 4
+    row = lambda v: v.reshape(1, -1)
+    ema = (
+        jnp.stack([ema_delta, ema_alpha, ema_beta, ema_gamma])
+        .transpose(0, 2, 1)
+        .reshape(4, NDIM, 8, 128)
+    )
+    backward_bias = jnp.concatenate([position_bias[:1], position_bias[:0:-1]])
+    small = [
+        tokens[0], out_grad[0], row(norm1_gain), row(norm1_bias), row(value_bias), ema,
+        ema_omega.reshape(8, 128), row(base_bias), shared_gamma, row(query_offset),
+        row(backward_bias), row(proj_bias), row(norm2_gain), row(norm2_bias), row(ffn1_bias),
+        row(ffn2_bias),
+    ]
+    large = [value_weight, base_weight, proj_weight, ffn1_weight, ffn2_weight]
+    f = lambda *shape: jax.ShapeDtypeStruct(shape, F32)
+    h = lambda *shape: jax.ShapeDtypeStruct(shape, BF)
+    outs = [
+        h(128, 1024), h(128, 1024), f(32, 2048), f(32, 4224), f(64, 1024), f(32, 4096), f(128, 1024),
+        f(SM_ROWS, 128), f(4, NDIM, 8, 128),
+    ]
+    vm = lambda *shape: pltpu.VMEM(shape, BF)
+    vf = lambda *shape: pltpu.VMEM(shape, F32)
+    dma = lambda *shape: pltpu.SemaphoreType.DMA(shape)
+    scratch = [
+        vm(1024, 1024), vm(1024, BASE_COLS), vm(1024, 1024), vm(1024, 1024), vm(1024, 1024),
+        vm(1024, 1024), vm(1024, 1024), vm(1024, 1024), vm(1024, 1152), vm(512, 1152),
+        vm(NZ, 64, 1024), vm(NZ, 64, 1024), vm(NZ, 64, 1024), vm(NZ, 64, 1152),
+        vm(NZ, 128, 1024), vm(NZ, 128, 1024),
+        vm(NZ - 1, 64, 1024), vm(NZ - 1, 64, 1024), vm(NZ - 1, 64, 1024), vm(NZ - 1, 64, 1152),
+        vm(NZ - 1, 128, 1024), vm(NZ - 1, 128, 1024),
+        vf(32, 1024), vf(32, BASE_COLS), vf(32, 1024), vf(32, BASE_COLS), vf(4, 32, 1024),
+        vm(32, 1024), vm(32, BASE_COLS), vm(256, 1024), vm(256, 1024), vm(1024, 1024),
+        vm(256, 1024), vm(256, 1024), vf(256, 1024), vf(128, 1024), vf(128, 1024), vf(256, 128),
+        vm(256, 1024), vm(256, 1024), vm(256, 1024), vf(256, 128), vf(128, 1024), vf(128, 1024),
+        vf(512, 1024), vm(1024, 1024),
+        vm(512, 1024), vm(256, 1024), vm(128, 1024), vm(128, 1024), vm(128, 1024),
+        vm(256, 1024), vm(128, 1024), vm(256, BASE_COLS), vm(256, 1024), vf(256, 128), vf(256, 128),
+        vm(256, 1024), vf(2, 128, 1024),
+        vf(1024, 128), vf(1024, 128), vf(1024, 128), vf(1024, 128), vf(16, NDIM, 8, 128), vf(8, 8, 8, 128),
+        vf(6, NDIM, 8, 128), vf(NDIM, 8, 128), vf(NDIM, 8, 128), vf(NZ - 1, NDIM, 8, 128),
+        vf(NDIM, 8, 128), vf(NDIM, 8, 128), vf(NZ - 1, NDIM, 8, 128),
+        vf(NDIM, 8, 128), vf(NDIM, 8, 128), vf(NDIM, 8, 128), vf(NDIM, 8, 128),
+        vf(SM_ROWS // 2, 128), vf(2, SM_ROWS // 2, 128), vf(2, SM_ROWS // 2, 128),
+        vf(NZ, SM_ROWS // 2, 128), vf(SM_ROWS // 2, 128),
+        dma(5), dma(5, NZ), dma(5, NZ), dma(5, NZ), dma(5, NZ), dma(3, 2, NZ), dma(3, 2, NZ),
+        dma(4, NZ, 2), dma(4, NZ, 2), dma(6, NZ), dma(6, NZ), dma(6, NZ), dma(6, NZ), dma(64), dma(64),
+    ]
+    (block_out, tokens_grad, dvalue, dbase, dproj, dffn1, dffn2, sums, dema) = pl.pallas_call(
+        functools.partial(layer_kernel, NS),
+        out_shape=outs,
+        in_specs=[pl.BlockSpec(memory_space=pltpu.VMEM)] * len(small)
+        + [pl.BlockSpec(memory_space=pl.ANY)] * len(large),
+        out_specs=[pl.BlockSpec(memory_space=pltpu.VMEM)] * len(outs),
+        scratch_shapes=scratch,
+        compiler_params=pltpu.CompilerParams(
+            collective_id=0, has_side_effects=True, vmem_limit_bytes=VMEM_LIMIT
+        ),
+    )(*small, *large)
+    dema = dema.reshape(4, NDIM, D).transpose(0, 2, 1)
+    span = lambda at, n: sums[at : at + n].reshape(-1)
+    dpos = span(ROW_POS, 1)
+    dposition = jnp.concatenate([dpos[:1], dpos[:0:-1]])
+    return (
+        block_out[None],
+        tokens_grad[None],
+        span(ROW_N1G, 8),
+        span(ROW_N1B, 8),
+        dvalue,
+        span(ROW_VB, 16),
+        dema[0],
+        dema[1],
+        dema[2],
+        dema[3],
+        span(ROW_OMEGA, 8),
+        dbase,
+        span(ROW_BB, 33),
+        sums[ROW_SG : ROW_SG + 2],
+        span(ROW_QO, 1),
+        dposition,
+        dproj,
+        span(ROW_PB, 8),
+        span(ROW_N2G, 8),
+        span(ROW_N2B, 8),
+        dffn1,
+        span(ROW_F1B, 32),
+        dffn2,
+        span(ROW_F2B, 8),
+    )
+
+
 def solution(mesh):
     in_specs = (
         P("batch", "seq", None),
@@ -431,4 +1637,7 @@
         P(("seq", "batch"), None),
         P(),
     )
-    return jax.shard_map(shards, mesh=mesh, in_specs=in_specs, out_specs=out_specs, check_vma=False)
+    one_device = fast_shards if mesh.shape['seq'] == 16 else shards
+    return jax.shard_map(
+        one_device, mesh=mesh, in_specs=in_specs, out_specs=out_specs, check_vma=False
+    )

time: 2900 us -> 386 us (0.13)
  waiting for transfers between devices: 1110 us -> 0 us
  local copies, waits for them, and re-layouts: 1110 us -> 21.5 us
  Pallas kernels: 0 us -> 358 us
  other arithmetic: 353 us -> 3.38 us
  matrix products: 185 us -> 0 us
  blocking collectives: 95.5 us -> 0 us
    reduce_scatter x5 -> x0, waiting for transfers between devices: 872 us -> none  [the longest x1 209 us: shards(): lax.psum_scatter(dbase_weight, ('seq', 'batch'), scatter_dimension=0, til...]
    reshape x16 -> x7, local copies, waits for them, and re-layouts: 370 us -> 8.85 us  [the longest x5 6.51 us: fast_shards(): span = lambda at, n: sums[at:at + n].reshape(-1)]
    pallas_call x0 -> x1, Pallas kernels: none -> 358 us  [fast_shards(): pl.pallas_call(functools.partial(layer_kernel, NS), out_shape=outs, in_sp...]
    psum x2 -> x0, waiting for transfers between devices: 238 us -> none  [shards(): lax.psum((dnorm1_gain, dnorm1_bias, dvalue_bias, dema_delta, dema_alpha,...]
    while x32 -> x0, local copies, waits for them, and re-layouts: 229 us -> none
    dot_general x31 -> x0, matrix products: 185 us -> none  [the longest x8 75.2 us: one_block(): return jnp.einsum('dts,bsd->btd', toeplitz, data_part, precision=precise)]
    gather x1 -> x0, local copies, waits for them, and re-layouts: 168 us -> none  [rel_table(): return jnp.where(offsets >= 0, position_bias[jnp.maximum(offsets, 0)], 0.0)]
    pad x16 -> x0, local copies, waits for them, and re-layouts: 141 us -> none  [the longest x8 88.9 us: toeplitz_rows(): return tiled.reshape(chans, block_len, 2 * block_len - 1)[:, :, :block_len]]
  transfers between devices with their start and end apart: 13 -> 0, of which waited for: 7 -> 0; matrix products, arithmetic and copies ran while one was open for 29% -> 0% of each run, Pallas kernels for 0% -> 0%
where the time goes in v1:
time: 386 us; the launch traced here: 384 us
  Pallas kernels  358 us (93%)
  local copies, waits for them, and re-layouts  21.5 us (6%)
    pallas_call x1, Pallas kernels, fast_shards(): pl.pallas_call(functools.partial(layer_kernel, NS), out_shape=outs, in_sp...  358 us
    unnamed x24, local copies, waits for them, and re-layouts  7.79 us

profile of v1, /device:TPU:27, one launch (start us, length us, event | category | flops | bytes accessed | tf_op | source)
XLA Modules:
  0.0 383.6 jit_solution(12044738408318562163)
XLA Ops:
  0.7 0.8 slice.70
  1.5 1.2 maximum_bitcast_fusion.refs_10_
  2.8 1.3 reshape.131.refs_7_
  4.1 0.9 pad_maximum_fusion
  5.0 0.8 copy.48
  5.8 358.1 %shard_map.415 = (bf16[128,1024]{1,0:T(8,128)(2,1)}, bf16[128,1024]{1,0:T(8,128)(2,1)}, f32[32,2048]{1,0:T(8,128)}, f32[32,4224]{1,0:T(8,128)}, f32[64,1024]{1,0...) custom-call(bf16[128,1024]{1,0:T(8,128)(2,1)} %bitcast.67, ...), custom_call_target="tpu_custom_call" | custom-call | tf_op jit(solution)/shard_map/pallas_call | solution.py:1544
  363.9 1.2 slice.82
  365.0 1.2 slice_bitcast_fusion.15
  366.2 0.8 slice_bitcast_fusion.14
  367.1 1.2 pad_maximum_fusion.1
  368.3 1.2 slice.80
  369.6 1.3 slice_bitcast_fusion.6
  370.9 1.3 slice_bitcast_fusion.5
  372.2 1.3 slice_bitcast_fusion.4
  373.5 1.4 slice_bitcast_fusion.7
  374.9 1.0 reshape.142
  375.9 0.7 slice_bitcast_fusion
  376.9 0.7 copy.56
  378.0 0.7 copy.57
  378.7 0.7 copy.58
  379.4 0.8 copy.59
  380.5 0.7 copy.60
  381.6 0.8 copy.61
  382.8 0.8 copy.62
  (18 shorter events, 2.0 us)
Async XLA Ops:
  0.7 3.4 copy-start.7
  375.9 1.0 copy-start.6
  376.9 1.0 copy-start.5
  376.9 1.7 copy-start.4
  378.0 1.4 copy-start
  379.4 1.1 copy-start.3
  380.5 1.1 copy-start.2
  381.6 1.2 copy-start.1

commit v2 on v1

--- a/solution.py
+++ b/solution.py
@@ -395,8 +395,13 @@
 ROW_OMEGA, ROW_N1G, ROW_N1B, ROW_N2G, ROW_N2B = 256, 264, 272, 280, 288
 ROW_VB, ROW_BB, ROW_PB, ROW_F1B, ROW_F2B = 296, 312, 345, 353, 385
 ROW_SG, ROW_QO, ROW_POS = 393, 395, 396
+SMALL_ROWS = (
+    (ROW_N1G, 8), (ROW_N1B, 8), (ROW_VB, 16), (ROW_OMEGA, 8), (ROW_BB, 33), (ROW_SG, 2), (ROW_QO, 1),
+    (ROW_POS, 1), (ROW_PB, 8), (ROW_N2G, 8), (ROW_N2B, 8), (ROW_F1B, 32), (ROW_F2B, 8),
+)
 VALUE, BASE, PROJ, FFN1, FFN2 = range(5)
 U_V, U_P, U_BA, U_BB, U_1, U_2 = range(6)
+Y_FIRST = (U_V,)
 
 
 def pick(flag, yes, no):
@@ -452,16 +457,19 @@
     NZ = NS // 4
     names = iter(refs)
     take = lambda n: [next(names) for _ in range(n)]
-    (tok, og, n1g, n1b, vb, ema, om, bb, sg, qo, pbr, pbias, n2g, n2b, f1b, f2b) = take(16)
+    (tok, og, n1g, n1b, vb) = take(5)
+    ema_in = take(4)
+    (om_in, bb, sg, qo, pbr, pbias, n2g, n2b, f1b, f2b) = take(10)
     (vw, bw, pw, f1w, f2w) = take(5)
-    (o_block, o_tok, o_dv, o_db, o_dp, o_d1, o_d2, o_sm, o_ema) = take(9)
+    (o_block, o_tok, o_dv, o_db, o_dp, o_d1, o_d2, o_ema, o_sm) = take(9)
+    (SM_OUT, ema, om) = take(3)
     (WV, WB, WP, W1, W2) = take(5)
     (G1, G2, GBA, GBB, RXBB) = take(5)
     RY = take(6)
     RZ = take(6)
     (FV, FB, FXV, FXB, FX1) = take(5)
     (SV, SB, NL, ML, NO, VP, VL, UH, UU, HH, SHP, RP, AD, GT, AT, PR, FO, FP, FG) = take(19)
-    (AS, AR, AX, AXR, OXR, GH, GUS, GBS, GA, GAT, GATR, GVP, GNVR) = take(13)
+    (AS, AR, AX, AXR, OX, OXR, OB, GH, GUS, GBS, GA, GAT, GATR, GVP, GNVR) = take(15)
     (XP, YP, GEP, GNP, HC, H8, EC, EXX, EXY, EXZ, BXX, BXY, BXZ, DEC, CIN, LAM, PIN) = take(17)
     (SMR, SMX, SMY, SMZ, SMC) = take(5)
     (in_sem, zs, zr, ys, yr, xs, xr, rxs, rxr, rys, ryr, rzs, rzr, es, er) = take(15)
@@ -498,7 +506,6 @@
     partners = [C, X, XC, Y] + [(ahead(k), b) for k in range(1, NZ)]
     for device in partners:
         pl.semaphore_signal(barrier, inc=1, device_id=device, device_id_type=MESH)
-    pl.semaphore_wait(barrier, len(partners))
 
     def remote(src, dst, send, recv, device):
         return pltpu.make_async_remote_copy(
@@ -538,20 +545,17 @@
             mine_ref[mine_rows, cols] = pick(first, lo, hi).astype(BF)
             other_ref[:, cols] = pick(first, hi, lo).astype(BF)
 
+    NT = NO.at[0:512]
+    OG = NO.at[512:1024]
+    quad = lambda j: rows_of(j, BLK)
+    q_c = q + 1 - 2 * b
+    q_x = lax.rem(q + 2, 4)
+    q_xc = lax.rem(q_c + 2, 4)
+    OG[quad(q), :] = og[...]
     loads[0].wait()
     split_columns(o_dv, 0, 8, WV, my_rows, 0, SV)
+    pl.semaphore_wait(barrier, len(partners))
     _, got_wv = exchange(SV, WV.at[my_rows], C, WV.at[other_rows])
-    loads[1].wait()
-    WB[my_rows, 0:512] = o_db[:, pl.ds(al(512 * b, 512), 512)].astype(BF)
-    SB[:, 0:512] = o_db[:, pl.ds(al(512 * (1 - b), 512), 512)].astype(BF)
-    WB[my_rows, 512:1024] = o_db[:, pl.ds(al(3200 + 512 * b, 128), 512)].astype(BF)
-    SB[:, 512:1024] = o_db[:, pl.ds(al(3200 + 512 * (1 - b), 128), 512)].astype(BF)
-    shared_cols = o_db[:, 1024:1152].astype(BF)
-    WB[my_rows, 1024:1152] = shared_cols
-    SB[:, 1024:1152] = shared_cols
-    split_columns(o_db, 1152, 8, WB, my_rows, 1152, SB)
-    _, got_wb = exchange(SB, WB.at[my_rows], C, WB.at[other_rows])
-
     gather = [WV, WB, WP, W1, W2]
 
     def piece(w, chip):
@@ -559,57 +563,60 @@
             return gather[w].at[rows_of(chip, 64)]
         return gather[w].at[rows_of(lax.div(chip, 2), 128)]
 
-    def send_z(w, k):
-        here = piece(w, s)
-        return remote(here, here, zs.at[w, k], zr.at[w, k], (ahead(k), b))
-
-    def got_z(w, k):
-        there = piece(w, behind(k))
-        return remote(there, there, zs.at[w, k], zr.at[w, k], (ahead(k), b))
-
-    def send_y(w, k):
-        part = piece(w, behind(k))
-        return remote(part, part, ys.at[w, k], yr.at[w, k], Y)
-
-    def got_y(w, k):
-        part = piece(w, ys_ + behind(k) - s)
-        return remote(part, part, ys.at[w, k], yr.at[w, k], Y)
-
-    def send_x(w, k, far):
-        chip = behind(k) if far == 0 else ys_ + behind(k) - s
-        part = piece(w, chip)
-        return remote(part, part, xs.at[w, far, k], xr.at[w, far, k], X)
-
-    def got_x(w, k, far):
-        chip = behind(k) if far == 0 else ys_ + behind(k) - s
-        part = piece(w, chip + xs_ - s)
-        return remote(part, part, xs.at[w, far, k], xr.at[w, far, k], X)
+    chip_of = lambda plane: 4 * plane + lax.rem(s, 4)
+
+    def send_z(w, plane, down):
+        part = piece(w, chip_of(plane))
+        device = (s - 4, b) if down else (s + 4, b)
+        return remote(part, part, zs.at[w, plane, down], zr.at[w, plane], device)
+
+    def send_y(w, plane):
+        part = piece(w, chip_of(plane))
+        return remote(part, part, ys.at[w, plane], yr.at[w, plane], Y)
+
+    def got_y(w, plane):
+        part = piece(w, chip_of(plane) + ys_ - s)
+        return remote(part, part, ys.at[w, plane], yr.at[w, plane], Y)
+
+    def send_x(w, plane, far):
+        part = piece(w, chip_of(plane) + (ys_ - s if far else 0))
+        return remote(part, part, xs.at[w, far, plane], xr.at[w, far, plane], X)
+
+    def got_x(w, plane, far):
+        part = piece(w, chip_of(plane) + (ys_ - s if far else 0) + xs_ - s)
+        return remote(part, part, xs.at[w, far, plane], xr.at[w, far, plane], X)
+
+    def near_planes(visit):
+        for j in range(1, NZ):
+            pl.when(z >= j)(functools.partial(visit, z - j, 0, z < NZ - 1))
+            pl.when(z + j <= NZ - 1)(functools.partial(visit, z + j, 1, z > 0))
 
     def open_gather(w):
-        for k in range(1, NZ):
-            send_z(w, k).start()
-        send_y(w, 0).start()
+        pl.when(z < NZ - 1)(lambda: send_z(w, z, 0).start())
+        pl.when(z > 0)(lambda: send_z(w, z, 1).start())
+        send_y(w, z).start()
         if w < FFN1:
-            send_x(w, 0, 0).start()
+            send_x(w, z, 0).start()
 
     def relay_z(w):
-        def one(k, carry):
-            got_z(w, k).wait_recv()
-            send_y(w, k).start()
+        def visit(plane, down, more):
+            part = piece(w, chip_of(plane))
+            remote(part, part, zs.at[w, plane, down], zr.at[w, plane], Y).wait_recv()
+            pl.when(more)(lambda: send_z(w, plane, down).start())
+            send_y(w, plane).start()
             if w < FFN1:
-                send_x(w, k, 0).start()
-            return carry
-
-        lax.fori_loop(1, NZ, one, 0)
+                send_x(w, plane, 0).start()
+
+        near_planes(visit)
 
     def relay_y(w):
-        def one(k, carry):
-            got_y(w, k).wait_recv()
+        def visit(plane, down, more):
+            got_y(w, plane).wait_recv()
             if w < FFN1:
-                send_x(w, k, 1).start()
-            return carry
-
-        lax.fori_loop(0, NZ, one, 0)
+                send_x(w, plane, 1).start()
+
+        visit(z, 0, False)
+        near_planes(visit)
 
     def finish_x(w):
         def one(k, carry):
@@ -629,11 +636,13 @@
 
         lax.fori_loop(0, NZ, one, 0)
 
-        def plane(k, carry):
-            send_z(w, k).wait_send()
-            return carry
-
-        lax.fori_loop(1, NZ, plane, 0)
+        pl.when(z < NZ - 1)(lambda: send_z(w, z, 0).wait_send())
+        pl.when(z > 0)(lambda: send_z(w, z, 1).wait_send())
+
+        def visit(plane, down, more):
+            pl.when(more)(lambda: send_z(w, plane, down).wait_send())
+
+        near_planes(visit)
 
     def norm_rows(v):
         center = v - jnp.mean(v, axis=-1, keepdims=True)
@@ -651,17 +660,11 @@
         NL[pl.ds(al(128 * b + 32 * i, 32), 32), :] = normed.astype(BF)
         return carry
 
-    got_wv.wait_recv()
-    open_gather(VALUE)
-    lax.fori_loop(0, 4, norm_one, 0)
-    _, got_nl = exchange(NL.at[own], NL.at[own], C, NL.at[rows_of(1 - b, BLK)])
-    got_wb.wait_recv()
-    open_gather(BASE)
-
-    NT = NO.at[0:512]
-    OG = NO.at[512:1024]
-    quad = lambda j: rows_of(j, BLK)
-
+    for g in range(8):
+        cols = slice(128 * g, 128 * g + 128)
+        om[g : g + 1, :] = om_in[:, cols]
+        for a in range(4):
+            ema[a, :, g, :] = ema_in[a][:, cols]
     for j in range(NDIM):
         rate = sig(ema[0, j])
         DEC[j] = 1.0 - rate * sig(ema[1, j])
@@ -688,35 +691,6 @@
         for j in range(NDIM):
             EC[0, j] = h[j]
 
-    end_scan()
-    _, got_ex = exchange(EC.at[0], EXX, X)
-
-    loads[2].wait()
-    WP[rows_of(s, 64), :] = o_dp[...].astype(BF)
-    loads[3].wait()
-    for j in range(4):
-        for t in range(8):
-            AS[32 * j : 32 * j + 32, 128 * t : 128 * t + 128] = o_d1[
-                :, 128 * (4 * t + j) : 128 * (4 * t + j) + 128
-            ].astype(BF)
-    f1_rows = lambda j: pl.ds(al(128 * p + 32 * j, 32), 32)
-    W1[f1_rows(q), :] = AS[rows_of(q, 32), :]
-    q_c = q + 1 - 2 * b
-    q_x = lax.rem(q + 2, 4)
-    q_xc = lax.rem(q_c + 2, 4)
-    f1_pairs = [
-        exchange(AS.at[rows_of(j, 32)], W1.at[f1_rows(q)], device, W1.at[f1_rows(j)])
-        for j, device in ((q_c, C), (q_x, X), (q_xc, XC))
-    ]
-    loads[4].wait()
-    W2[rows_of(p, 128), :] = o_d2[...].astype(BF)
-    OG[quad(q), :] = og[...]
-    copy_og_c, got_og_c = exchange(OG.at[quad(q)], OG.at[quad(q)], C, OG.at[quad(q_c)])
-    copy_og_x, got_og_x = exchange(OG.at[quad(q)], OG.at[quad(q)], X, OG.at[quad(q_x)])
-
-    open_gather(PROJ)
-    relay_z(VALUE)
-    relay_y(VALUE)
 
     def scan_round_x(own_state, arrived, out, incoming, later):
         for j in range(NDIM):
@@ -746,24 +720,61 @@
                 hop = hop * l4
             incoming[j] = total
 
+    loads[1].wait()
+    WB[my_rows, 0:512] = o_db[:, pl.ds(al(512 * b, 512), 512)].astype(BF)
+    SB[:, 0:512] = o_db[:, pl.ds(al(512 * (1 - b), 512), 512)].astype(BF)
+    WB[my_rows, 512:1024] = o_db[:, pl.ds(al(3200 + 512 * b, 128), 512)].astype(BF)
+    SB[:, 512:1024] = o_db[:, pl.ds(al(3200 + 512 * (1 - b), 128), 512)].astype(BF)
+    shared_cols = o_db[:, 1024:1152].astype(BF)
+    WB[my_rows, 1024:1152] = shared_cols
+    SB[:, 1024:1152] = shared_cols
+    split_columns(o_db, 1152, 8, WB, my_rows, 1152, SB)
+    _, got_wb = exchange(SB, WB.at[my_rows], C, WB.at[other_rows])
+
+    copy_og_x, got_og_x = exchange(OG.at[quad(q)], OG.at[quad(q)], X, OG.at[quad(q_x)])
+    loads[2].wait()
+    WP[rows_of(s, 64), :] = o_dp[...].astype(BF)
+    open_gather(PROJ)
+    got_wv.wait_recv()
+    open_gather(VALUE)
+    lax.fori_loop(0, 4, norm_one, 0)
+    _, got_nl = exchange(NL.at[own], NL.at[own], C, NL.at[rows_of(1 - b, BLK)])
+    end_scan()
+    _, got_ex = exchange(EC.at[0], EXX, X)
+    got_wb.wait_recv()
+    open_gather(BASE)
+    loads[4].wait()
+    W2[rows_of(p, 128), :] = o_d2[...].astype(BF)
+    open_gather(FFN2)
+
     got_ex.wait_recv()
     scan_round_x(EC.at[0], EXX, EC.at[1], PIN, x == 1)
     _, got_ey = exchange(EC.at[1], EXY, Y)
+    loads[3].wait()
+    for j in range(4):
+        for t in range(8):
+            AS[32 * j : 32 * j + 32, 128 * t : 128 * t + 128] = o_d1[
+                :, 128 * (4 * t + j) : 128 * (4 * t + j) + 128
+            ].astype(BF)
+    f1_rows = lambda j: pl.ds(al(128 * p + 32 * j, 32), 32)
+    W1[f1_rows(q), :] = AS[rows_of(q, 32), :]
+    f1_pairs = [
+        exchange(AS.at[rows_of(j, 32)], W1.at[f1_rows(q)], device, W1.at[f1_rows(j)])
+        for j, device in ((q_c, C), (q_x, X), (q_xc, XC))
+    ]
+    copy_og_c, got_og_c = exchange(OG.at[quad(q)], OG.at[quad(q)], C, OG.at[quad(q_c)])
+    got_ey.wait_recv()
+    scan_round_y(EC.at[1], EXY, EC.at[2], PIN, y == 1, x)
+    got_ez = [exchange(EC.at[2], EXZ.at[k - 1], (ahead(k), b))[1] for k in range(1, NZ)]
     for copy, got in f1_pairs:
         copy.wait_send()
         settle(copy)
         got.wait_recv()
     open_gather(FFN1)
+    relay_z(VALUE)
+    relay_y(VALUE)
     relay_z(BASE)
-    got_ey.wait_recv()
-    scan_round_y(EC.at[1], EXY, EC.at[2], PIN, y == 1, x)
-    got_ez = [exchange(EC.at[2], EXZ.at[k - 1], (ahead(k), b))[1] for k in range(1, NZ)]
-    open_gather(FFN2)
     relay_y(BASE)
-    got_og_x.wait_recv()
-    copy_og_xc, got_og_xc = exchange(OG.at[quad(q_x)], OG.at[quad(q_x)], C, OG.at[quad(q_xc)])
-    relay_z(PROJ)
-    relay_y(PROJ)
     for got in got_ez:
         got.wait_recv()
     scan_round_z(EXZ, PIN, z, 2 * y + x)
@@ -804,6 +815,8 @@
 
     lax.fori_loop(0, 4, mixed_one, 0)
     _, got_ml = exchange(ML.at[own], ML.at[own], C, ML.at[rows_of(1 - b, BLK)])
+    relay_z(PROJ)
+    relay_y(PROJ)
 
     low_row = low1(1)
 
@@ -828,6 +841,7 @@
         VL[:, cols] = silu(v).astype(BF)
 
     relay_z(FFN1)
+    relay_z(FFN2)
 
     got_ml.wait_recv()
     finish_x(BASE)
@@ -853,7 +867,7 @@
         sh = shared_of(i)
         return (sh * sg[0:1, :] + qo[...]).astype(BF), (sh * sg[1:2, :]).astype(BF)
 
-    position = shear(jnp.broadcast_to(pbr[...], (BLK, BLK)), False)
+    position = jnp.transpose(shear(jnp.broadcast_to(pbr[...], (BLK, BLK)), False))
     at_row = lax.broadcasted_iota(jnp.int32, (BLK, BLK), 0)
     at_col = lax.broadcasted_iota(jnp.int32, (BLK, BLK), 1)
     causal = at_row >= at_col
@@ -871,8 +885,6 @@
             AD[rows, cols] = att.astype(BF)
             GT[rows, cols] = (att * silu(RP[rows, cols].astype(F32))).astype(BF)
 
-    relay_z(FFN2)
-
     finish_x(PROJ)
     copy_u.wait_send()
     copy_h.wait_send()
@@ -899,6 +911,8 @@
         return carry
 
     lax.fori_loop(0, 4, residual_one, 0)
+    got_og_x.wait_recv()
+    copy_og_xc, got_og_xc = exchange(OG.at[quad(q_x)], OG.at[quad(q_x)], C, OG.at[quad(q_xc)])
     copy_nt_x, got_nt_x = exchange(NT.at[quad(q)], NT.at[quad(q)], X, NT.at[quad(q_x)])
     copy_nt_c, got_nt_c = exchange(NT.at[quad(q)], NT.at[quad(q)], C, NT.at[quad(q_c)])
 
@@ -954,14 +968,10 @@
         lax.fori_loop(0, 4, one, 0)
         return exchange(out, out_landing, X)
 
-    def reduced(staged, landing, out_landing, i):
+    def pair_sum(staged, landing, i):
         mine = pl.ds(al(128 * q + 32 * i, 32), 32)
         got = pl.ds(al(128 * x + 32 * i, 32), 32)
-        return (
-            staged[mine, :].astype(F32)
-            + landing[got, :].astype(F32)
-            + out_landing[rows_of(i, 32), :].astype(F32)
-        )
+        return staged[mine, :].astype(F32) + landing[got, :].astype(F32)
 
     got_a = reduce_pair(AS, AR)
 
@@ -969,7 +979,6 @@
         for g in range(v.shape[1] // 128):
             SM_OUT[row + g : row + g + 1, :] = v[:, 128 * g : 128 * g + 128]
 
-    SM_OUT = o_sm
     SM_OUT[...] = jnp.zeros((SM_ROWS, 128), F32)
 
     def weight_grad(left, right, out, right0, out0, width):
@@ -992,16 +1001,23 @@
             return rows_of(chip, 64)
         return rows_of(lax.div(chip, 2), 128)
 
+    y_first = Y_FIRST
+    hop_x, hop_y = xs_ - s, ys_ - s
+
+    def hops(u):
+        return (hop_y, hop_x, Y, X) if u in y_first else (hop_x, hop_y, X, Y)
+
     def rs_x(u, k, far):
-        plane = ahead(k)
-        chip = plane if far == 0 else plane + ys_ - s
-        src = grads[u].at[shard(u, chip + xs_ - s)]
+        hop1, hop2, device, _ = hops(u)
+        chip = ahead(k) + (hop2 if far else 0)
+        src = grads[u].at[shard(u, chip + hop1)]
         slot = half[u].at[pl.ds(al(64 * (2 * k + far), 64), 64)]
-        return remote(src, slot, rxs.at[u, k, far], rxr.at[u, k, far], X)
+        return remote(src, slot, rxs.at[u, k, far], rxr.at[u, k, far], device)
 
     def rs_y(u, k):
-        src = grads[u].at[shard(u, ahead(k) + ys_ - s)]
-        return remote(src, RY[u].at[k], rys.at[u, k], ryr.at[u, k], Y)
+        _, hop2, _, device = hops(u) if u < U_1 else (0, hop_y, X, Y)
+        src = grads[u].at[shard(u, ahead(k) + hop2)]
+        return remote(src, RY[u].at[k], rys.at[u, k], ryr.at[u, k], device)
 
     def rs_z(u, k):
         src = grads[u].at[shard(u, ahead(k))]
@@ -1009,7 +1025,7 @@
 
     turn = lambda i: lax.rem(i + 1, NZ)
 
-    def rs_open(u):
+    def rs_open(u, start=0, stop=None):
         def one(i, carry):
             k = turn(i)
             if u < U_1:
@@ -1019,25 +1035,23 @@
                 rs_y(u, k).start()
             return carry
 
-        lax.fori_loop(0, NZ, one, 0)
-
-    def rs_pass_x(u):
+        lax.fori_loop(start, NZ if stop is None else stop, one, 0)
+
+    def rs_pass_x(u, start=0, stop=None):
         def one(i, carry):
             k = turn(i)
-            plane = ahead(k)
             for far in (1, 0):
                 rs_x(u, k, far).wait_recv()
-                chip = plane if far == 0 else plane + ys_ - s
-                rows = shard(u, chip)
+                rows = shard(u, ahead(k) + (hops(u)[1] if far else 0))
                 got = half[u][pl.ds(al(64 * (2 * k + far), 64), 64), :]
                 grads[u][rows, :] = (grads[u][rows, :].astype(F32) + got.astype(F32)).astype(BF)
                 if far == 1:
                     rs_y(u, k).start()
             return carry
 
-        lax.fori_loop(0, NZ, one, 0)
-
-    def rs_pass_y(u):
+        lax.fori_loop(start, NZ if stop is None else stop, one, 0)
+
+    def rs_pass_y(u, start=0, stop=None):
         def one(i, carry):
             k = i + 1
             rs_y(u, k).wait_recv()
@@ -1046,8 +1060,9 @@
             rs_z(u, k).start()
             return carry
 
-        lax.fori_loop(0, NZ - 1, one, 0)
-        rs_y(u, 0).wait_recv()
+        lax.fori_loop(start, NZ - 1 if stop is None else stop, one, 0)
+        if stop is None:
+            rs_y(u, 0).wait_recv()
 
     def rs_total(u, rows_in):
         rows = shard(u, s)
@@ -1074,20 +1089,9 @@
         acc = lax.fori_loop(0, ref.shape[0] // 32, one, jnp.zeros((8, width), F32))
         return jnp.sum(acc, axis=0, keepdims=True)
 
-    weight_grad(FL, OG, G2, 0, 0, 1024)
-    rs_open(U_2)
-    a_x = reduce_x(AS, AR, got_a, AX, AXR)
-    weight_grad(NT, GF, G1, 0, 0, 1024)
-    rs_open(U_1)
-    f1_sum = column_sum(GF, 0, 1024)
-    for t in range(8):
-        SM_OUT[pl.ds(ROW_F1B + 4 * t + q, 1), :] = f1_sum[:, 128 * t : 128 * t + 128]
-
-    a_x[1].wait_recv()
-
     def back_two(i, carry):
         rows = rows_of(i, 32)
-        a = reduced(AS, AR, AXR, i)
+        a = pair_sum(AS, AR, i) + AXR[rows, :].astype(F32)
         n, rstd = norm_rows(FO[rows, :])
         g = a * n2g[...]
         grad = og[rows, :].astype(F32) + (
@@ -1108,6 +1112,32 @@
             carry[3] + fold8(og[rows, :].astype(F32)),
         )
 
+    weight_grad(FL, OG, G2, 0, 0, 1024)
+    rs_open(U_2)
+    close_gather(FFN1)
+    a_x = reduce_x(AS, AR, got_a, AX, AXR)
+    for m in range(2):
+        for n in range(2):
+            rows = slice(256 * m, 256 * m + 256)
+            cols = slice(512 * n, 512 * n + 512)
+            FP[rows, cols] = dot_nn(FL[rows, :], W2[:, cols])
+    got_o = reduce_pair(FP, GNVR)
+    close_gather(FFN2)
+    weight_grad(NT, GF, G1, 0, 0, 1024)
+    rs_open(U_1, 0, 2)
+    f1_sum = column_sum(GF, 0, 1024)
+    for t in range(8):
+        SM_OUT[pl.ds(ROW_F1B + 4 * t + q, 1), :] = f1_sum[:, 128 * t : 128 * t + 128]
+    o_x = reduce_x(FP, GNVR, got_o, OX, OXR)
+
+    def out_one(i, carry):
+        OB[rows_of(i, 32), :] = pair_sum(FP, GNVR, i)
+        return carry
+
+    lax.fori_loop(0, 4, out_one, 0)
+    rs_pass_y(U_2, 0, 1)
+
+    a_x[1].wait_recv()
     zero8 = jnp.zeros((8, 1024), F32)
     sums = lax.fori_loop(0, 4, back_two, (zero8, zero8, zero8, zero8))
     _, got_gh = exchange(GH.at[own], GH.at[own], C, GH.at[theirs])
@@ -1115,20 +1145,14 @@
     GBS[own, 0:512] = GUS[:, my_cols]
     for row, acc in zip((ROW_N2G, ROW_N2B, ROW_PB, ROW_F2B), sums):
         store_row(row, jnp.sum(acc, axis=0, keepdims=True))
+    rs_pass_y(U_2, 1, 2)
 
     got_gh.wait_recv()
-    for copy, _ in got_a:
-        copy.wait_send()
-        settle(copy)
-    for m in range(2):
-        for n in range(2):
-            rows = slice(256 * m, 256 * m + 256)
-            cols = slice(512 * n, 512 * n + 512)
-            AS[rows, cols] = dot_nn(FL[rows, :], W2[:, cols]).astype(BF)
-    got_o = reduce_pair(AS, AR)
-    close_gather(FFN1)
-    close_gather(FFN2)
-
+    got_gu.wait_recv()
+    GBS[:, 512:1024] = GH[:, my_cols]
+    weight_grad(ML, GBS, GBA, 0, 0, 1024)
+    o_x[1].wait_recv()
+    rs_open(U_BA)
     for n in range(2):
         cols = slice(512 * n, 512 * n + 512)
         gg = dot_nt(GH[...], WP[cols, :])
@@ -1142,9 +1166,7 @@
         rows = slice(128 * i, 128 * i + 128)
         GAT[rows, :] = dot_nt(GA[rows, :], VL[rows, :])
     _, got_gat = exchange(GAT, GATR, C)
-    a_x[0].wait_send()
-    settle(a_x[0])
-    o_x = reduce_x(AS, AR, got_o, AX, OXR)
+    weight_grad(GT, GH, FG, 0, 0, 1024)
     for i in range(2):
         rows = slice(128 * i, 128 * i + 128)
         low = AT[rows, :].astype(BF)
@@ -1152,10 +1174,6 @@
             cols = slice(512 * n, 512 * n + 512)
             gv = dot_tn(low, GA[rows, cols])
             GVP[rows, cols] = (gv * slope(VP[rows, cols].astype(F32))).astype(BF)
-    GBS[:, 512:1024] = GH[:, my_cols]
-    o_x[1].wait_recv()
-    weight_grad(GT, GH, FG, 0, 0, 1024)
-    rs_open(U_P)
     got_gat.wait_recv()
     for i in range(2):
         rows = slice(128 * i, 128 * i + 128)
@@ -1167,7 +1185,8 @@
         gk = dot_tn(gs, qs) * SCALE
         pre = SHP[rows, :]
         sh = silu(pre)
-        GBS[rows, 1024:1152] = ((gq * sg[0:1, :] + gk * sg[1:2, :]) * slope(pre)).astype(BF)
+        gsp = (gq * sg[0:1, :] + gk * sg[1:2, :]) * slope(pre)
+        GBS[rows, 1024:1152] = (gsp * 0.5).astype(BF)
         mine = b == i
 
         @pl.when(mine)
@@ -1176,14 +1195,69 @@
             SM_OUT[ROW_SG + 1 : ROW_SG + 2, :] = jnp.sum(gk * sh, axis=0, keepdims=True)
             SM_OUT[ROW_QO : ROW_QO + 1, :] = jnp.sum(gq, axis=0, keepdims=True)
             SM_OUT[ROW_POS : ROW_POS + 1, :] = jnp.sum(
-                shear(gs.astype(F32), True), axis=0, keepdims=True
+                shear(jnp.transpose(gs.astype(F32)), True), axis=0, keepdims=True
             )
 
-    got_gu.wait_recv()
-    weight_grad(ML, GBS, GBA, 0, 0, 1024)
-    rs_open(U_BA)
+    GM = FP.at[0:256]
+    GNV = FP.at[256:512]
+    for copy, _ in got_o:
+        copy.wait_send()
+        settle(copy)
+    for n in range(2):
+        cols = slice(512 * n, 512 * n + 512)
+        GM[:, cols] = dot_nt(GBS[...], WB[cols, :])
+    _, got_gm = exchange(GM.at[theirs], GNVR.at[0:128], C)
+    for n in range(2):
+        cols = slice(512 * n, 512 * n + 512)
+        GNV[:, cols] = dot_nt(GVP[...], WV[cols, :])
+    _, got_gnv = exchange(GNV.at[theirs], GNVR.at[128:256], C)
+    GBS[:, 1024:1152] = (GBS[:, 1024:1152].astype(F32) * 2.0).astype(BF)
+    rs_pass_y(U_2, 2)
+
+    def grad_ema_one(i, carry):
+        for g in range(8):
+            cols = slice(128 * g, 128 * g + 128)
+            rows = pl.ds(al(128 * g + 32 * i, 32), 32)
+            v = GM[pl.ds(al(128 * b + 32 * i, 32), 32), cols] + GNVR[rows_of(i, 32), cols]
+            GEP[rows, :] = v * slope(YP[rows, :])
+        return carry
+
+    def adjoint_end():
+        d = [DEC[j] for j in range(NDIM)]
+
+        def step(i, g):
+            row = GEP[panel(BLK - 1 - i), :]
+            return tuple(g[j] * d[j] + row for j in range(NDIM))
+
+        g = lax.fori_loop(
+            0, BLK, step, tuple(jnp.zeros((8, 128), F32) for _ in range(NDIM)), unroll=4
+        )
+        for j in range(NDIM):
+            EC[3, j] = g[j]
+
+    got_gm.wait_recv()
+    lax.fori_loop(0, 4, grad_ema_one, 0)
+    adjoint_end()
+    _, got_bx = exchange(EC.at[3], BXX, X)
+    rs_open(U_P)
+    rs_pass_x(U_BA, 0, 2)
+    got_bx.wait_recv()
+    scan_round_x(EC.at[3], BXX, EC.at[4], PIN, x == 0)
+    _, got_by = exchange(EC.at[4], BXY, Y)
+    rs_open(U_1, 2)
+    for copy in (copy_og_c, copy_og_x, copy_og_xc, copy_nt_x, copy_nt_c, copy_nt_xc):
+        copy.wait_send()
+        settle(copy)
+    weight_grad(NL, GVP, NO, 0, 0, 1024)
+    rs_pass_y(U_1, 0, 2)
+    rs_pass_x(U_BA, 2)
+    got_by.wait_recv()
+    scan_round_y(EC.at[4], BXY, EC.at[5], PIN, y == 0, 1 - x)
+    got_bz = [
+        exchange(EC.at[5], BXZ.at[k - 1], (ahead(NZ - k), b))[1] for k in range(1, NZ)
+    ]
+    rs_open(U_V)
     weight_grad(ML, GBS, GBB, 1024, 0, 1152)
-    rs_open(U_BB)
     base_sum = column_sum(GBS, 0, BASE_COLS)
     for t in range(4):
         cols = slice(128 * t, 128 * t + 128)
@@ -1202,73 +1276,21 @@
             SM_OUT[row + 2 * t + 1 : row + 2 * t + 2, :] = keep * pick(first, turned, block)
 
     store_half(ROW_BB + 9, base_sum[:, 1152:2176])
-    GBS[:, 1024:1152] = (GBS[:, 1024:1152].astype(F32) * 0.5).astype(BF)
-    GM = FP.at[0:256]
-    GNV = FP.at[256:512]
-    for n in range(2):
-        cols = slice(512 * n, 512 * n + 512)
-        GM[:, cols] = dot_nt(GBS[...], WB[cols, :])
-    _, got_gm = exchange(GM.at[theirs], GNVR.at[0], C)
-    for n in range(2):
-        cols = slice(512 * n, 512 * n + 512)
-        GNV[:, cols] = dot_nt(GVP[...], WV[cols, :])
-    _, got_gnv = exchange(GNV.at[theirs], GNVR.at[1], C)
-    for copy in (copy_og_c, copy_og_x, copy_og_xc, copy_nt_x, copy_nt_c, copy_nt_xc):
-        copy.wait_send()
-        settle(copy)
-    weight_grad(NL, GVP, NO, 0, 0, 1024)
-    rs_open(U_V)
     store_half(ROW_VB, column_sum(GVP, 0, 1024))
-
-    got_gm.wait_recv()
-
-    def grad_ema_one(i, carry):
-        for g in range(8):
-            cols = slice(128 * g, 128 * g + 128)
-            rows = pl.ds(al(128 * g + 32 * i, 32), 32)
-            v = GM[pl.ds(al(128 * b + 32 * i, 32), 32), cols] + GNVR[0, rows_of(i, 32), cols]
-            GEP[rows, :] = v * slope(YP[rows, :])
-        return carry
-
-    lax.fori_loop(0, 4, grad_ema_one, 0)
-
-    def adjoint_end():
-        d = [DEC[j] for j in range(NDIM)]
-
-        def step(i, g):
-            row = GEP[panel(BLK - 1 - i), :]
-            return tuple(g[j] * d[j] + row for j in range(NDIM))
-
-        g = lax.fori_loop(
-            0, BLK, step, tuple(jnp.zeros((8, 128), F32) for _ in range(NDIM)), unroll=4
-        )
-        for j in range(NDIM):
-            EC[3, j] = g[j]
-
-    adjoint_end()
-    _, got_bx = exchange(EC.at[3], BXX, X)
-    rs_pass_y(U_2)
-    got_bx.wait_recv()
-    scan_round_x(EC.at[3], BXX, EC.at[4], PIN, x == 0)
-    _, got_by = exchange(EC.at[4], BXY, Y)
-    rs_pass_y(U_1)
-    got_by.wait_recv()
-    scan_round_y(EC.at[4], BXY, EC.at[5], PIN, y == 0, 1 - x)
-    got_bz = [
-        exchange(EC.at[5], BXZ.at[k - 1], (ahead(NZ - k), b))[1] for k in range(1, NZ)
-    ]
-    rs_pass_x(U_P)
 
     def block_out_one(i, carry):
         rows = rows_of(i, 32)
-        o_block[rows, :] = (FO[rows, :] + (reduced(AS, AR, OXR, i) + f2b[...])).astype(BF)
+        o_block[rows, :] = (
+            FO[rows, :] + ((OB[rows, :] + OXR[rows, :].astype(F32)) + f2b[...])
+        ).astype(BF)
         return carry
 
     lax.fori_loop(0, 4, block_out_one, 0)
+    rs_pass_y(U_BA, 0, 2)
     for got in got_bz:
         got.wait_recv()
     scan_round_z(BXZ, PIN, NZ - 1 - z, 2 * (1 - y) + 1 - x)
-
+    rs_pass_y(U_1, 2)
     def backward_scan():
         for part in range(2):
             js = range(8 * part, 8 * part + 8)
@@ -1310,6 +1332,8 @@
                 SM_OUT[128 + 8 * j : 128 + 8 * j + 8, :] = m[n]
 
     backward_scan()
+    rs_pass_y(U_BA, 2)
+    rs_pass_x(U_P, 0, 2)
 
     for g in range(8):
         rows = slice(128 * g, 128 * g + 128)
@@ -1324,7 +1348,7 @@
         wide = jnp.concatenate(
             [GNP[pl.ds(al(128 * g + 32 * i, 32), 32), :] for g in range(8)], axis=1
         )
-        a = (GNV[pl.ds(al(128 * b + 32 * i, 32), 32), :] + GNVR[1, rows, :]) + wide
+        a = (GNV[pl.ds(al(128 * b + 32 * i, 32), 32), :] + GNVR[pl.ds(al(128 + 32 * i, 32), 32), :]) + wide
         n, rstd = norm_rows(tok[rows, :].astype(F32))
         g = a * n1g[...]
         back = (
@@ -1341,20 +1365,21 @@
     my_part = rows_of(b, half_rows)
     their_part = rows_of(1 - b, half_rows)
     copy_c, got_c = exchange(SM_OUT.at[their_part], SMR, C)
-    rs_pass_x(U_BA)
+    rs_pass_x(U_P, 2)
     got_c.wait_recv()
     SMX[0] = SM_OUT[my_part, :] + SMR[...]
     _, got_sx = exchange(SMX.at[0], SMX.at[1], X)
-    rs_pass_y(U_P)
+    rs_open(U_BB)
+    rs_pass_y(U_P, 0, 2)
     got_sx.wait_recv()
     SMY[0] = SMX[0] + SMX[1]
     _, got_sy = exchange(SMY.at[0], SMY.at[1], Y)
-    rs_pass_y(U_BA)
+    rs_pass_x(U_V)
+    rs_pass_y(U_P, 2)
     got_sy.wait_recv()
     SMZ[0] = SMY[0] + SMY[1]
     got_sz = [exchange(SMZ.at[0], SMZ.at[k], (ahead(k), b))[1] for k in range(1, NZ)]
     rs_pass_x(U_BB)
-    rs_pass_x(U_V)
     for got in got_sz:
         got.wait_recv()
     total = SMZ[lax.rem(z, NZ)]
@@ -1363,8 +1388,8 @@
     SM_OUT[my_part, :] = total
     _, got_cc = exchange(SM_OUT.at[my_part], SMC, C)
 
+    rs_pass_y(U_V)
     rs_pass_y(U_BB)
-    rs_pass_y(U_V)
     rs_wait_z(U_2)
     for i in range(4):
         o_d2[32 * i : 32 * i + 32, :] = rs_total(U_2, (32 * i, 32))
@@ -1433,6 +1458,7 @@
         o_ema[2, j] = gamma * rate * s1
         o_ema[3, j] = EMA_SCALE * rate * beta * s1
 
+    o_sm[...] = SM_OUT[...]
     got_ba.wait_recv()
     o_db[:, their_cols] = FXB[:, 0:512]
     o_db[:, h_their] = FXB[:, 512:1024]
@@ -1464,6 +1490,21 @@
 
     for u in (U_V, U_P, U_BA, U_BB, U_1, U_2):
         close_sums(u)
+
+
+def hand_on_kernel(*refs):
+    large, (ema, sums), outs = refs[:7], refs[7:9], refs[9:]
+    for src, dst in zip(large, outs):
+        dst[...] = src[...]
+    for a in range(4):
+        for g in range(8):
+            outs[7 + a][:, 128 * g : 128 * g + 128] = ema[a, :, g, :]
+    for out, (row, n) in zip(outs[11:], SMALL_ROWS):
+        if out.shape[0] == 1:
+            for g in range(n):
+                out[:, 128 * g : 128 * g + 128] = sums[row + g : row + g + 1, :]
+        else:
+            out[...] = sums[row : row + n, :]
 
 
 def fast_shards(
@@ -1495,16 +1536,11 @@
     NS = lax.axis_size("seq")
     NZ = NS // 4
     row = lambda v: v.reshape(1, -1)
-    ema = (
-        jnp.stack([ema_delta, ema_alpha, ema_beta, ema_gamma])
-        .transpose(0, 2, 1)
-        .reshape(4, NDIM, 8, 128)
-    )
-    backward_bias = jnp.concatenate([position_bias[:1], position_bias[:0:-1]])
     small = [
-        tokens[0], out_grad[0], row(norm1_gain), row(norm1_bias), row(value_bias), ema,
-        ema_omega.reshape(8, 128), row(base_bias), shared_gamma, row(query_offset),
-        row(backward_bias), row(proj_bias), row(norm2_gain), row(norm2_bias), row(ffn1_bias),
+        tokens[0], out_grad[0], row(norm1_gain), row(norm1_bias), row(value_bias),
+        ema_delta.T, ema_alpha.T, ema_beta.T, ema_gamma.T,
+        row(ema_omega), row(base_bias), shared_gamma, row(query_offset),
+        row(position_bias), row(proj_bias), row(norm2_gain), row(norm2_bias), row(ffn1_bias),
         row(ffn2_bias),
     ]
     large = [value_weight, base_weight, proj_weight, ffn1_weight, ffn2_weight]
@@ -1512,12 +1548,14 @@
     h = lambda *shape: jax.ShapeDtypeStruct(shape, BF)
     outs = [
         h(128, 1024), h(128, 1024), f(32, 2048), f(32, 4224), f(64, 1024), f(32, 4096), f(128, 1024),
-        f(SM_ROWS, 128), f(4, NDIM, 8, 128),
+        f(4, NDIM, 8, 128),
     ]
+    outs.append(f(SM_ROWS, 128))
     vm = lambda *shape: pltpu.VMEM(shape, BF)
     vf = lambda *shape: pltpu.VMEM(shape, F32)
     dma = lambda *shape: pltpu.SemaphoreType.DMA(shape)
     scratch = [
+        vf(SM_ROWS, 128), vf(4, NDIM, 8, 128), vf(8, 128),
         vm(1024, 1024), vm(1024, BASE_COLS), vm(1024, 1024), vm(1024, 1024), vm(1024, 1024),
         vm(1024, 1024), vm(1024, 1024), vm(1024, 1024), vm(1024, 1152), vm(512, 1152),
         vm(NZ, 64, 1024), vm(NZ, 64, 1024), vm(NZ, 64, 1024), vm(NZ, 64, 1152),
@@ -1529,19 +1567,19 @@
         vm(256, 1024), vm(256, 1024), vf(256, 1024), vf(128, 1024), vf(128, 1024), vf(256, 128),
         vm(256, 1024), vm(256, 1024), vm(256, 1024), vf(256, 128), vf(128, 1024), vf(128, 1024),
         vf(512, 1024), vm(1024, 1024),
-        vm(512, 1024), vm(256, 1024), vm(128, 1024), vm(128, 1024), vm(128, 1024),
+        vm(512, 1024), vm(256, 1024), vm(128, 1024), vm(128, 1024), vm(128, 1024), vm(128, 1024), vf(128, 1024),
         vm(256, 1024), vm(128, 1024), vm(256, BASE_COLS), vm(256, 1024), vf(256, 128), vf(256, 128),
-        vm(256, 1024), vf(2, 128, 1024),
+        vm(256, 1024), vf(256, 1024),
         vf(1024, 128), vf(1024, 128), vf(1024, 128), vf(1024, 128), vf(16, NDIM, 8, 128), vf(8, 8, 8, 128),
         vf(6, NDIM, 8, 128), vf(NDIM, 8, 128), vf(NDIM, 8, 128), vf(NZ - 1, NDIM, 8, 128),
         vf(NDIM, 8, 128), vf(NDIM, 8, 128), vf(NZ - 1, NDIM, 8, 128),
         vf(NDIM, 8, 128), vf(NDIM, 8, 128), vf(NDIM, 8, 128), vf(NDIM, 8, 128),
         vf(SM_ROWS // 2, 128), vf(2, SM_ROWS // 2, 128), vf(2, SM_ROWS // 2, 128),
         vf(NZ, SM_ROWS // 2, 128), vf(SM_ROWS // 2, 128),
-        dma(5), dma(5, NZ), dma(5, NZ), dma(5, NZ), dma(5, NZ), dma(3, 2, NZ), dma(3, 2, NZ),
+        dma(5), dma(5, NZ, 2), dma(5, NZ), dma(5, NZ), dma(5, NZ), dma(3, 2, NZ), dma(3, 2, NZ),
         dma(4, NZ, 2), dma(4, NZ, 2), dma(6, NZ), dma(6, NZ), dma(6, NZ), dma(6, NZ), dma(64), dma(64),
     ]
-    (block_out, tokens_grad, dvalue, dbase, dproj, dffn1, dffn2, sums, dema) = pl.pallas_call(
+    results = pl.pallas_call(
         functools.partial(layer_kernel, NS),
         out_shape=outs,
         in_specs=[pl.BlockSpec(memory_space=pltpu.VMEM)] * len(small)
@@ -1552,35 +1590,45 @@
             collective_id=0, has_side_effects=True, vmem_limit_bytes=VMEM_LIMIT
         ),
     )(*small, *large)
-    dema = dema.reshape(4, NDIM, D).transpose(0, 2, 1)
-    span = lambda at, n: sums[at : at + n].reshape(-1)
-    dpos = span(ROW_POS, 1)
-    dposition = jnp.concatenate([dpos[:1], dpos[:0:-1]])
+    final = list(outs[:7]) + [f(NDIM, D)] * 4
+    final += [f(2, 128) if row == ROW_SG else f(1, 128 * n) for row, n in SMALL_ROWS]
+    local = pl.BlockSpec(memory_space=pltpu.VMEM)
+    (block_out, tokens_grad, dvalue, dbase, dproj, dffn1, dffn2, ddelta, dalpha, dbeta, dgamma, *sums) = (
+        pl.pallas_call(
+            hand_on_kernel,
+            out_shape=final,
+            in_specs=[local] * 9,
+            out_specs=[local] * len(final),
+        )(*results)
+    )
+    (dn1g, dn1b, dvb, dom, dbb, dsg, dqo, dpos, dpb, dn2g, dn2b, df1b, df2b) = [
+        v if v.shape[0] == 2 else v.reshape(-1) for v in sums
+    ]
     return (
         block_out[None],
         tokens_grad[None],
-        span(ROW_N1G, 8),
-        span(ROW_N1B, 8),
+        dn1g,
+        dn1b,
         dvalue,
-        span(ROW_VB, 16),
-        dema[0],
-        dema[1],
-        dema[2],
-        dema[3],
-        span(ROW_OMEGA, 8),
+        dvb,
+        ddelta.T,
+        dalpha.T,
+        dbeta.T,
+        dgamma.T,
+        dom,
         dbase,
-        span(ROW_BB, 33),
-        sums[ROW_SG : ROW_SG + 2],
-        span(ROW_QO, 1),
-        dposition,
+        dbb,
+        dsg,
+        dqo,
+        dpos,
         dproj,
-        span(ROW_PB, 8),
-        span(ROW_N2G, 8),
-        span(ROW_N2B, 8),
+        dpb,
+        dn2g,
+        dn2b,
         dffn1,
-        span(ROW_F1B, 32),
+        df1b,
         dffn2,
-        span(ROW_F2B, 8),
+        df2b,
     )
 
 

time: 386 us -> 285 us (0.74)
  Pallas kernels: 358 us -> 279 us
  local copies, waits for them, and re-layouts: 21.5 us -> 2.05 us
    pallas_call x1, Pallas kernels: 358 us -> 275 us  [fast_shards(): pl.pallas_call(functools.partial(layer_kernel, NS), out_shape=outs, in_sp...]
    reshape x6 -> x0, local copies, waits for them, and re-layouts: 7.5 us -> none  [the longest x5 6.51 us: fast_shards(): span = lambda at, n: sums[at:at + n].reshape(-1)]
    unnamed x24 -> x4, local copies, waits for them, and re-layouts: 7.79 us -> 1.43 us
    slice x4 -> x0, local copies, waits for them, and re-layouts: 3.95 us -> none  [the longest x2 1.94 us: fast_shards(): dposition = jnp.concatenate([dpos[:1], dpos[:0:-1]])]
where the time goes in v2:
time: 285 us; the launch traced here: 282 us
  Pallas kernels  279 us (98%)
    pallas_call x1, Pallas kernels, fast_shards(): pl.pallas_call(functools.partial(layer_kernel, NS), out_shape=outs, in_sp...  275 us

profile of v2, /device:TPU:27, one launch (start us, length us, event | category | flops | bytes accessed | tf_op | source)
XLA Modules:
  0.0 282.1 jit_solution(10364921594896572623)
XLA Ops:
  0.7 0.0 copy-start
  0.7 0.7 copy-done
  1.4 0.6 reshape.124.refs_10_
  2.0 275.2 %shard_map.415 = (bf16[128,1024]{1,0:T(8,128)(2,1)}, bf16[128,1024]{1,0:T(8,128)(2,1)}, f32[32,2048]{1,0:T(8,128)}, f32[32,4224]{1,0:T(8,128)}, f32[64,1024]{1,0...) custom-call(bf16[128,1024]{1,0:T(8,128)(2,1)} %bitcast.34, ...), custom_call_target="tpu_custom_call" | custom-call | tf_op jit(solution)/shard_map/pallas_call | solution.py:1582
  277.2 3.5 %shard_map.416 = (bf16[128,1024]{1,0:T(8,128)(2,1)}, bf16[128,1024]{1,0:T(8,128)(2,1)}, f32[32,2048]{1,0:T(8,128)}, f32[32,4224]{1,0:T(8,128)}, f32[64,1024]{1,0...) custom-call(bf16[128,1024]{1,0:T(8,128)(2,1)} %get-tuple-element.57., ...), custom_call_target="tpu_custom_call" | custom-call | tf_op jit(solution)/shard_map/pallas_call | solution.py:1597
  280.7 0.0 copy-start.1
  280.7 0.7 copy-done.1
  281.4 0.6 reduce
Async XLA Ops:
  0.7 0.7 copy-start
  280.7 0.7 copy-start.1

commit v3 on v2

--- a/solution.py
+++ b/solution.py
@@ -402,6 +402,7 @@
 VALUE, BASE, PROJ, FFN1, FFN2 = range(5)
 U_V, U_P, U_BA, U_BB, U_1, U_2 = range(6)
 Y_FIRST = (U_V,)
+X_THEN_Y = (VALUE,)
 
 
 def pick(flag, yes, no):
@@ -565,49 +566,60 @@
 
     chip_of = lambda plane: 4 * plane + lax.rem(s, 4)
 
-    def send_z(w, plane, down):
-        part = piece(w, chip_of(plane))
+    def route(w):
+        return (xs_ - s, ys_ - s, X, Y) if w in X_THEN_Y else (ys_ - s, xs_ - s, Y, X)
+
+    def send_z(w, plane, down, side=0):
+        part = piece(w, chip_of(plane) + (ys_ - s if side else 0))
         device = (s - 4, b) if down else (s + 4, b)
-        return remote(part, part, zs.at[w, plane, down], zr.at[w, plane], device)
+        return remote(part, part, zs.at[w, plane, down, side], zr.at[w, plane, side], device)
+
+    def got_z(w, plane, side=0):
+        part = piece(w, chip_of(plane) + (ys_ - s if side else 0))
+        return remote(part, part, zs.at[w, plane, 0, side], zr.at[w, plane, side], Y)
 
     def send_y(w, plane):
         part = piece(w, chip_of(plane))
-        return remote(part, part, ys.at[w, plane], yr.at[w, plane], Y)
+        return remote(part, part, ys.at[w, plane], yr.at[w, plane], route(w)[2])
 
     def got_y(w, plane):
-        part = piece(w, chip_of(plane) + ys_ - s)
-        return remote(part, part, ys.at[w, plane], yr.at[w, plane], Y)
+        part = piece(w, chip_of(plane) + route(w)[0])
+        return remote(part, part, ys.at[w, plane], yr.at[w, plane], route(w)[2])
 
     def send_x(w, plane, far):
-        part = piece(w, chip_of(plane) + (ys_ - s if far else 0))
-        return remote(part, part, xs.at[w, far, plane], xr.at[w, far, plane], X)
+        part = piece(w, chip_of(plane) + (route(w)[0] if far else 0))
+        return remote(part, part, xs.at[w, far, plane], xr.at[w, far, plane], route(w)[3])
 
     def got_x(w, plane, far):
-        part = piece(w, chip_of(plane) + (ys_ - s if far else 0) + xs_ - s)
-        return remote(part, part, xs.at[w, far, plane], xr.at[w, far, plane], X)
-
-    def near_planes(visit):
-        for j in range(1, NZ):
+        part = piece(w, chip_of(plane) + (route(w)[0] if far else 0) + route(w)[1])
+        return remote(part, part, xs.at[w, far, plane], xr.at[w, far, plane], route(w)[3])
+
+    def near_planes(visit, start=1, stop=NZ):
+        for j in range(start, stop):
             pl.when(z >= j)(functools.partial(visit, z - j, 0, z < NZ - 1))
             pl.when(z + j <= NZ - 1)(functools.partial(visit, z + j, 1, z > 0))
 
+    def spread_z(w, side=0):
+        pl.when(z < NZ - 1)(lambda: send_z(w, z, 0, side).start())
+        pl.when(z > 0)(lambda: send_z(w, z, 1, side).start())
+
     def open_gather(w):
-        pl.when(z < NZ - 1)(lambda: send_z(w, z, 0).start())
-        pl.when(z > 0)(lambda: send_z(w, z, 1).start())
         send_y(w, z).start()
+        spread_z(w)
         if w < FFN1:
             send_x(w, z, 0).start()
 
-    def relay_z(w):
+    def relay_z(w, start=1, stop=NZ):
         def visit(plane, down, more):
-            part = piece(w, chip_of(plane))
-            remote(part, part, zs.at[w, plane, down], zr.at[w, plane], Y).wait_recv()
-            pl.when(more)(lambda: send_z(w, plane, down).start())
-            send_y(w, plane).start()
+            for side in range(2 if w == FFN2 else 1):
+                got_z(w, plane, side).wait_recv()
+                pl.when(more)(lambda side=side: send_z(w, plane, down, side).start())
+            if w < FFN2:
+                send_y(w, plane).start()
             if w < FFN1:
                 send_x(w, plane, 0).start()
 
-        near_planes(visit)
+        near_planes(visit, start, stop)
 
     def relay_y(w):
         def visit(plane, down, more):
@@ -616,7 +628,10 @@
                 send_x(w, plane, 1).start()
 
         visit(z, 0, False)
-        near_planes(visit)
+        if w < FFN2:
+            near_planes(visit)
+        else:
+            spread_z(w, 1)
 
     def finish_x(w):
         def one(k, carry):
@@ -634,15 +649,18 @@
                 send_x(w, k, 1).wait_send()
             return carry
 
-        lax.fori_loop(0, NZ, one, 0)
-
-        pl.when(z < NZ - 1)(lambda: send_z(w, z, 0).wait_send())
-        pl.when(z > 0)(lambda: send_z(w, z, 1).wait_send())
-
-        def visit(plane, down, more):
-            pl.when(more)(lambda: send_z(w, plane, down).wait_send())
-
-        near_planes(visit)
+        if w < FFN2:
+            lax.fori_loop(0, NZ, one, 0)
+        else:
+            send_y(w, z).wait_send()
+        for side in range(2 if w == FFN2 else 1):
+            pl.when(z < NZ - 1)(lambda side=side: send_z(w, z, 0, side).wait_send())
+            pl.when(z > 0)(lambda side=side: send_z(w, z, 1, side).wait_send())
+
+            def visit(plane, down, more, side=side):
+                pl.when(more)(lambda: send_z(w, plane, down, side).wait_send())
+
+            near_planes(visit)
 
     def norm_rows(v):
         center = v - jnp.mean(v, axis=-1, keepdims=True)
@@ -772,6 +790,7 @@
         got.wait_recv()
     open_gather(FFN1)
     relay_z(VALUE)
+    relay_y(FFN2)
     relay_y(VALUE)
     relay_z(BASE)
     relay_y(BASE)
@@ -840,8 +859,8 @@
         VP[:, cols] = v.astype(BF)
         VL[:, cols] = silu(v).astype(BF)
 
-    relay_z(FFN1)
-    relay_z(FFN2)
+    relay_z(FFN1, 1, 3)
+    relay_z(FFN2, 1, 2)
 
     got_ml.wait_recv()
     finish_x(BASE)
@@ -861,6 +880,9 @@
             dot_nn(ML[...], WB[:, 1152 + 512 * n : 1664 + 512 * n]) + rbias[:, 512 * n : 512 * n + 512]
         ).astype(BF)
 
+    relay_z(FFN1, 3)
+    relay_z(FFN2, 2, 3)
+
     shared_of = lambda i: silu(SHP[128 * i : 128 * i + 128, :])
 
     def queries_keys(i):
@@ -885,6 +907,8 @@
             AD[rows, cols] = att.astype(BF)
             GT[rows, cols] = (att * silu(RP[rows, cols].astype(F32))).astype(BF)
 
+    relay_z(FFN2, 3)
+
     finish_x(PROJ)
     copy_u.wait_send()
     copy_h.wait_send()
@@ -917,7 +941,6 @@
     copy_nt_c, got_nt_c = exchange(NT.at[quad(q)], NT.at[quad(q)], C, NT.at[quad(q_c)])
 
     relay_y(FFN1)
-    relay_y(FFN2)
     got_og_c.wait_recv()
     got_og_xc.wait_recv()
     for m in range(2):
@@ -1258,6 +1281,7 @@
     ]
     rs_open(U_V)
     weight_grad(ML, GBS, GBB, 1024, 0, 1152)
+    rs_open(U_BB, 0, 2)
     base_sum = column_sum(GBS, 0, BASE_COLS)
     for t in range(4):
         cols = slice(128 * t, 128 * t + 128)
@@ -1369,27 +1393,18 @@
     got_c.wait_recv()
     SMX[0] = SM_OUT[my_part, :] + SMR[...]
     _, got_sx = exchange(SMX.at[0], SMX.at[1], X)
-    rs_open(U_BB)
+    rs_open(U_BB, 2)
     rs_pass_y(U_P, 0, 2)
+    rs_pass_x(U_BB, 0, 2)
     got_sx.wait_recv()
     SMY[0] = SMX[0] + SMX[1]
     _, got_sy = exchange(SMY.at[0], SMY.at[1], Y)
     rs_pass_x(U_V)
     rs_pass_y(U_P, 2)
+    rs_pass_x(U_BB, 2)
     got_sy.wait_recv()
     SMZ[0] = SMY[0] + SMY[1]
     got_sz = [exchange(SMZ.at[0], SMZ.at[k], (ahead(k), b))[1] for k in range(1, NZ)]
-    rs_pass_x(U_BB)
-    for got in got_sz:
-        got.wait_recv()
-    total = SMZ[lax.rem(z, NZ)]
-    for k in range(1, NZ):
-        total = total + SMZ[lax.rem(z + NZ - k, NZ)]
-    SM_OUT[my_part, :] = total
-    _, got_cc = exchange(SM_OUT.at[my_part], SMC, C)
-
-    rs_pass_y(U_V)
-    rs_pass_y(U_BB)
     rs_wait_z(U_2)
     for i in range(4):
         o_d2[32 * i : 32 * i + 32, :] = rs_total(U_2, (32 * i, 32))
@@ -1401,9 +1416,6 @@
         exchange(o_d1.at[:, quarter(j)], FX1.at[q], device, FX1.at[j])
         for j, device in ((q_c, C), (q_x, X), (q_xc, XC))
     ]
-    rs_wait_z(U_P)
-    for i in range(2):
-        o_dp[32 * i : 32 * i + 32, :] = rs_total(U_P, (32 * i, 32))
     mine32 = 32 * b
     their32 = 32 * (1 - b)
     h_mine = pl.ds(al(3200 + 512 * b, 128), 512)
@@ -1425,25 +1437,20 @@
     part = rs_total(U_BA, (mine32, 32))
     o_db[:, my_cols] = part[:, 0:512]
     o_db[:, h_mine] = part[:, 512:1024]
-    rs_wait_z(U_BB)
-    FB[:, 1024:2176] = rs_total(U_BB, (their32, 32))
-    _, got_bb = exchange(FB.at[:, 1024:2176], FXB.at[:, 1024:2176], C)
-    part = rs_total(U_BB, (mine32, 32))
-    o_db[:, 1024:1152] = part[:, 0:128]
-    rs_wait_z(U_V)
-    FV[...] = rs_total(U_V, (their32, 32))
-    _, got_v = exchange(FV, FXV, C)
-    part_v = rs_total(U_V, (mine32, 32))
-
-    FX1[q] = o_d1[:, quarter(q)]
-    for copy, got in d1_pairs:
-        copy.wait_send()
-        settle(copy)
+    rs_pass_y(U_V)
+    rs_pass_y(U_BB, 0, 2)
+    for got in got_sz:
         got.wait_recv()
-    for j in range(4):
-        for t in range(8):
-            o_d1[:, 128 * (4 * t + j) : 128 * (4 * t + j) + 128] = FX1[j, :, 128 * t : 128 * t + 128]
-
+    total = SMZ[lax.rem(z, NZ)]
+    for k in range(1, NZ):
+        total = total + SMZ[lax.rem(z + NZ - k, NZ)]
+    SM_OUT[my_part, :] = total
+    _, got_cc = exchange(SM_OUT.at[my_part], SMC, C)
+
+    rs_wait_z(U_P)
+    for i in range(2):
+        o_dp[32 * i : 32 * i + 32, :] = rs_total(U_P, (32 * i, 32))
+    rs_pass_y(U_BB, 2)
     copy_c.wait_send()
     settle(copy_c)
     got_cc.wait_recv()
@@ -1459,9 +1466,28 @@
         o_ema[3, j] = EMA_SCALE * rate * beta * s1
 
     o_sm[...] = SM_OUT[...]
+    rs_wait_z(U_V)
+    FV[...] = rs_total(U_V, (their32, 32))
+    _, got_v = exchange(FV, FXV, C)
+    part_v = rs_total(U_V, (mine32, 32))
+
     got_ba.wait_recv()
     o_db[:, their_cols] = FXB[:, 0:512]
     o_db[:, h_their] = FXB[:, 512:1024]
+    FX1[q] = o_d1[:, quarter(q)]
+    for copy, got in d1_pairs:
+        copy.wait_send()
+        settle(copy)
+        got.wait_recv()
+    for j in range(4):
+        for t in range(8):
+            o_d1[:, 128 * (4 * t + j) : 128 * (4 * t + j) + 128] = FX1[j, :, 128 * t : 128 * t + 128]
+
+    rs_wait_z(U_BB)
+    FB[:, 1024:2176] = rs_total(U_BB, (their32, 32))
+    _, got_bb = exchange(FB.at[:, 1024:2176], FXB.at[:, 1024:2176], C)
+    part = rs_total(U_BB, (mine32, 32))
+    o_db[:, 1024:1152] = part[:, 0:128]
     got_bb.wait_recv()
     merge(o_db, 1152, part[:, 128:1152], FXB[:, 1152:2176])
     got_v.wait_recv()
@@ -1576,7 +1602,7 @@
         vf(NDIM, 8, 128), vf(NDIM, 8, 128), vf(NDIM, 8, 128), vf(NDIM, 8, 128),
         vf(SM_ROWS // 2, 128), vf(2, SM_ROWS // 2, 128), vf(2, SM_ROWS // 2, 128),
         vf(NZ, SM_ROWS // 2, 128), vf(SM_ROWS // 2, 128),
-        dma(5), dma(5, NZ, 2), dma(5, NZ), dma(5, NZ), dma(5, NZ), dma(3, 2, NZ), dma(3, 2, NZ),
+        dma(5), dma(5, NZ, 2, 2), dma(5, NZ, 2), dma(5, NZ), dma(5, NZ), dma(3, 2, NZ), dma(3, 2, NZ),
         dma(4, NZ, 2), dma(4, NZ, 2), dma(6, NZ), dma(6, NZ), dma(6, NZ), dma(6, NZ), dma(64), dma(64),
     ]
     results = pl.pallas_call(

time: 285 us -> 275 us (0.965)
  Pallas kernels: 279 us -> 271 us
    pallas_call x1, Pallas kernels: 275 us -> 268 us  [fast_shards(): pl.pallas_call(functools.partial(layer_kernel, NS), out_shape=outs, in_sp...]
where the time goes in v3:
time: 275 us
  Pallas kernels  271 us (99%)
    pallas_call x1, Pallas kernels, fast_shards(): pl.pallas_call(functools.partial(layer_kernel, NS), out_shape=outs, in_sp...  268 us

profile of v3, /device:TPU:27, one launch (start us, length us, event | category | flops | bytes accessed | tf_op | source)
XLA Modules:
  0.0 274.9 jit_solution(6339172882159541164)
XLA Ops:
  0.7 0.0 copy-start
  0.7 0.7 copy-done
  1.4 0.6 reshape.124.refs_10_
  2.0 268.0 %shard_map.415 = (bf16[128,1024]{1,0:T(8,128)(2,1)}, bf16[128,1024]{1,0:T(8,128)(2,1)}, f32[32,2048]{1,0:T(8,128)}, f32[32,4224]{1,0:T(8,128)}, f32[64,1024]{1,0...) custom-call(bf16[128,1024]{1,0:T(8,128)(2,1)} %bitcast.34, ...), custom_call_target="tpu_custom_call" | custom-call | tf_op jit(solution)/shard_map/pallas_call | solution.py:1608
  270.0 3.5 %shard_map.416 = (bf16[128,1024]{1,0:T(8,128)(2,1)}, bf16[128,1024]{1,0:T(8,128)(2,1)}, f32[32,2048]{1,0:T(8,128)}, f32[32,4224]{1,0:T(8,128)}, f32[64,1024]{1,0...) custom-call(bf16[128,1024]{1,0:T(8,128)(2,1)} %get-tuple-element.57., ...), custom_call_target="tpu_custom_call" | custom-call | tf_op jit(solution)/shard_map/pallas_call | solution.py:1623
  273.5 0.0 copy-start.1
  273.5 0.7 copy-done.1
  274.2 0.6 reduce
Async XLA Ops:
  0.7 0.7 copy-start
  273.5 0.7 copy-start.1

commit v4 on v3

--- a/solution.py
+++ b/solution.py
@@ -794,6 +794,7 @@
     relay_y(VALUE)
     relay_z(BASE)
     relay_y(BASE)
+    relay_z(PROJ)
     for got in got_ez:
         got.wait_recv()
     scan_round_z(EXZ, PIN, z, 2 * y + x)
@@ -834,7 +835,6 @@
 
     lax.fori_loop(0, 4, mixed_one, 0)
     _, got_ml = exchange(ML.at[own], ML.at[own], C, ML.at[rows_of(1 - b, BLK)])
-    relay_z(PROJ)
     relay_y(PROJ)
 
     low_row = low1(1)

time: 275 us -> 272 us (0.989)
  no operation moved by 1% of the time
where the time goes in v4:
time: 272 us
  Pallas kernels  269 us (99%)
    pallas_call x1, Pallas kernels, fast_shards(): pl.pallas_call(functools.partial(layer_kernel, NS), out_shape=outs, in_sp...  265 us

profile of v4, /device:TPU:27, one launch (start us, length us, event | category | flops | bytes accessed | tf_op | source)
XLA Modules:
  0.0 272.1 jit_solution(5874119111297241198)
XLA Ops:
  0.7 0.0 copy-start
  0.7 0.7 copy-done
  1.4 0.6 reshape.124.refs_10_
  2.0 265.3 %shard_map.415 = (bf16[128,1024]{1,0:T(8,128)(2,1)}, bf16[128,1024]{1,0:T(8,128)(2,1)}, f32[32,2048]{1,0:T(8,128)}, f32[32,4224]{1,0:T(8,128)}, f32[64,1024]{1,0...) custom-call(bf16[128,1024]{1,0:T(8,128)(2,1)} %bitcast.34, ...), custom_call_target="tpu_custom_call" | custom-call | tf_op jit(solution)/shard_map/pallas_call | solution.py:1608
  267.3 3.5 %shard_map.416 = (bf16[128,1024]{1,0:T(8,128)(2,1)}, bf16[128,1024]{1,0:T(8,128)(2,1)}, f32[32,2048]{1,0:T(8,128)}, f32[32,4224]{1,0:T(8,128)}, f32[64,1024]{1,0...) custom-call(bf16[128,1024]{1,0:T(8,128)(2,1)} %get-tuple-element.57., ...), custom_call_target="tpu_custom_call" | custom-call | tf_op jit(solution)/shard_map/pallas_call | solution.py:1623
  270.8 0.0 copy-start.1
  270.8 0.7 copy-done.1
  271.5 0.6 reduce
Async XLA Ops:
  0.7 0.7 copy-start
  270.8 0.7 copy-start.1
